TPU v7x, 32 devices: a whole 2x2x4 slice. The times are simulated.
32 devices in a mesh: groups: 2 (over y), pair: 4 (over z), mm: 2 (over x), sub: 2 (over core).
Axes of the slice: x: 2, y: 2, z: 4, core: 2. Of those that a mesh axis runs over, the one named last changes fastest.
Arguments:
- centers: float32 [256, 3, 128], P(('groups', 'pair', 'sub')), parts along dimension 0, may hold values from -6 to 6
- widths: float32 [256, 128], P(('groups', 'pair', 'sub')), parts along dimension 0, may hold values from 0.2 to 2
- density: float32 [256, 128], P(('groups', 'pair', 'sub')), parts along dimension 0, may hold values from -0.3 to 0.3
- prefactor: float32 [256, 128], P(('groups', 'pair', 'sub')), parts along dimension 0, may hold values from 0.2 to 2
- padding: int32 [256], P(('groups', 'pair', 'sub')), parts along dimension 0, may hold values from 0 to 64
- pattern: int32 [256, 2, 16], P(('groups', 'pair', 'sub'), 'mm'), parts along dimension 0, may hold values from 0 to 255, as said below
- mm_coords: float32 [512, 2, 3, 128], P(('groups', 'pair'), 'mm'), parts along dimension 0, may hold values from -6 to 6
- mm_charges: float32 [512, 2, 128], P(('groups', 'pair'), 'mm'), parts along dimension 0, may hold values from -1 to 1
Outputs:
- mm_force: float32 [512, 2, 3, 128], P(('groups', 'pair'), 'mm'), parts along dimension 0
- tile_force: float32 [256, 3, 128], P(('groups', 'pair', 'sub')), parts along dimension 0
There are 2 independent parts, one for each index of `groups`. A program takes and returns all parts, laid end to end along the dimension named above; each array names one. Nothing has to cross between parts.
Inputs may be any that keep to these rules, and one draw needn't show every extreme that they name: `pattern`: values index the 256 blocks of the slot's MM group and may repeat within a tile. Block b belongs to pair index b // 64. Among the 256 slots of one device's tiles (an aligned run of 16 tiles) for one MM group, at most 128 name blocks of one pair index, and in each such run some pair index is named exactly 128 times.
All inputs are finite; a program needn't handle non-finite values.
Results may differ from a plain program's by a relative error of at most 0.00016.
Values sent between devices are 32-bit elements; how exact they have to be, the bound alone decides.
A program may use at most 64 MiB of HBM per device.

v0:
```python
import math

import jax
import jax.numpy as jnp
from jax import lax
from jax.sharding import PartitionSpec as P


def interact(centers, widths, weight, coords, charges):
    delta_sq = jnp.sum((coords[:, None, :] - centers[:, :, None]) ** 2, axis=0)
    coef = weight[:, None] * charges[None, :] * (delta_sq + widths[:, None]) ** (-1.5)
    col_total = jnp.sum(coef, axis=0)
    row_total = jnp.sum(coef, axis=1)
    cross_atoms = jnp.dot(centers, coef, precision=lax.Precision.HIGHEST)
    cross_pairs = jnp.dot(coords, coef.T, precision=lax.Precision.HIGHEST)
    mm_term = coords * col_total[None, :] - cross_atoms
    center_term = centers * row_total[None, :] - cross_pairs
    return (mm_term, center_term)


def evaluate_items(package, coords, charges):
    items = package.shape[0]
    group = math.gcd(items, 32)
    package = package.reshape((items // group, group) + package.shape[1:])
    coords = coords.reshape((items // group, group) + coords.shape[1:])
    charges = charges.reshape((items // group, group) + charges.shape[1:])

    def one_group(args):
        pkg, crd, chg = args
        return jax.vmap(interact)(pkg[:, 0:3], pkg[:, 3], pkg[:, 4], crd, chg)

    mm_term, center_term = lax.map(one_group, (package, coords, charges))
    return (
        mm_term.reshape((items,) + mm_term.shape[2:]),
        center_term.reshape((items,) + center_term.shape[2:]),
    )


def body(centers, widths, density, prefactor, padding, pattern, mm_coords, mm_charges):
    tiles_dev = centers.shape[0]
    pairs = centers.shape[2]
    near = pattern.shape[2]
    owned = mm_coords.shape[0]
    atoms = mm_coords.shape[3]
    slots = jnp.arange(pairs, dtype=jnp.int32)[None, :]
    weight = jnp.where(slots < (pairs - padding)[:, None], density * prefactor, jnp.float32(0.0))
    package = jnp.concatenate([centers, widths[:, None, :], weight[:, None, :]], axis=1)
    blocks = pattern[:, 0, :].reshape(-1)
    tile_of = jnp.repeat(jnp.arange(tiles_dev, dtype=jnp.int32), near)
    coords_here = mm_coords[:, 0]
    charges_here = mm_charges[:, 0]
    all_coords, all_charges = (
        lax.all_gather(coords_here, "pair", axis=0, tiled=True),
        lax.all_gather(charges_here, "pair", axis=0, tiled=True),
    )
    mm_terms, center_terms = evaluate_items(
        package[tile_of], all_coords[blocks], all_charges[blocks]
    )
    inside = (blocks >= 0) & (blocks < owned * lax.axis_size("pair"))
    target = jnp.where(inside, blocks, owned * lax.axis_size("pair"))
    mm_part = lax.psum_scatter(
        jnp.zeros((owned * lax.axis_size("pair"), 3, atoms), jnp.float32)
        .at[target]
        .add(mm_terms, mode="drop"),
        "pair",
        scatter_dimension=0,
        tiled=True,
    )
    tile_part = jnp.sum(center_terms.reshape(tiles_dev, near, 3, pairs), axis=1)
    mm_force = lax.psum(mm_part, "sub")[:, None]
    tile_force = lax.psum(tile_part, "mm")
    return (mm_force, tile_force)


def solution(mesh):
    placed = (
        P(("groups", "pair", "sub"), None, None),
        P(("groups", "pair", "sub"), None),
        P(("groups", "pair", "sub"), None),
        P(("groups", "pair", "sub"), None),
        P(("groups", "pair", "sub")),
        P(("groups", "pair", "sub"), "mm", None),
        P(("groups", "pair"), "mm", None, None),
        P(("groups", "pair"), "mm", None),
    )
    return jax.shard_map(
        body,
        mesh=mesh,
        in_specs=placed,
        out_specs=(
            P(("groups", "pair"), "mm", None, None),
            P(("groups", "pair", "sub"), None, None),
        ),
        check_vma=False,
    )
```

profile of v0, /device:TPU:0, one launch (start us, length us, event | category | flops | bytes accessed | tf_op | source)
XLA Modules:
  0.0 211.9 jit_solution(9561945370943612420)
XLA Ops:
  7.2 0.0 all-reduce.6.cloned.1.call-start
  7.3 0.5 broadcast.112
  7.8 1.4 reduce.3
  9.2 0.1 reshape_squeeze.3
  9.3 0.9 copy.31
  10.2 16.2 %all-gather = f32[256,1,3,128]{3,0,2,1:T(8,128)S(1)} all-gather(f32[64,1,3,128]{3,0,2,1:T(8,128)S(1)} %copy.31), channel_id=2, replica_groups=mesh['groups'=2,'pair'=4,'mm'=2,'sub'=2] {'pair'}, dimensions={0}, use_global_device_ids=true | all-gather | bytes 491520 | tf_op jit(solution)/shard_map/all_gather | solution.py:53
  26.4 0.3 copy.32
  26.7 14.0 %all-gather.1 = f32[256,1,128]{2,0,1:T(8,128)S(1)} all-gather(f32[64,1,128]{2,0,1:T(8,128)} %bitcast.69), channel_id=3, replica_groups=mesh['groups'=2,'pair'=4,'mm'=2,'sub'=2] {'pair'}, dimensions={0}, use_global_device_ids=true | all-gather | bytes 163840 | tf_op jit(solution)/shard_map/all_gather | solution.py:54
  40.7 1.0 gather_fusion
  41.7 0.7 gather_fusion.2
  42.5 0.1 reshape.126
  42.6 0.1 multiply_select_fusion
  42.7 1.0 gather_fusion.1
  43.7 90.0 %while.12 = (s32[]{:T(128)}, f32[8,32,3,128]{3,2,1,0:T(4,128)S(1)}, f32[8,32,3,128]{3,2,1,0:T(4,128)S(1)}, f32[8,32,3,128]{3,2,1,0:T(4,128)S(1)}, f32[8,32,5,128...) while((s32[]{:T(128)}, f32[8,32,3,128]{3,2,1,0:T(4,128)S(1)}, f32[8,32,3,128]{3,2,1,0:T(4,128)S(1)}, ...), condition=%wide.region_4.5_spmd, body=%wide.region_0.4_spmd.sunk | while | flops 47751168 | bytes 9552989 | solution.py:32
  43.8 2.1 multiply_reduce_fusion.2
  46.0 1.9 fusion.17
  47.8 4.2 %fusion.19 = f32[8,32,3,128]{3,2,1,0:T(4,128)S(1)} fusion(f32[8,32,3,128]{3,2,1,0:T(4,128)S(1)} %get-tuple-element.123, s32[]{:T(128)} %get-tuple-element.121, f32[32,128,128]{2,1,0:T(8,128)S(1)} %multiply_reduce_fusion.2, f32[32,128]{1,0:T(8,128)S(1)} %bitcast.59, f32[32,128]{1,0:T(8,128)S(1)} %dynamic-slice_bitcast_fusion.11, ...), kind=kOutput, calls=%fused_computation.8.clone.1 | convolution fusion | flops 20471808 | bytes 2360320 | tf_op jit(solution)/shard_map/while/body/eval_jaxpr/vmap()/dot_general | solution.py:15
  52.1 2.9 %fusion.18 = f32[8,32,3,128]{3,2,1,0:T(4,128)S(1)} fusion(f32[8,32,3,128]{3,2,1,0:T(4,128)S(1)} %get-tuple-element.122, s32[]{:T(128)} %get-tuple-element.121, f32[32,128,128]{2,1,0:T(8,128)S(1)} %multiply_reduce_fusion.2, f32[32,128]{1,0:T(8,128)S(1)} %bitcast.60, f32[32,128]{1,0:T(8,128)S(1)} %dynamic-slice_bitcast_fusion.11, ...), kind=kOutput, calls=%fused_computation.11.clone.1 | convolution fusion | flops 20471808 | bytes 2359300 | tf_op jit(solution)/shard_map/while/body/eval_jaxpr/vmap()/dot_general | solution.py:14
  55.1 2.1 multiply_reduce_fusion.2
  57.2 1.9 fusion.17
  59.1 4.2 %fusion.19 = f32[8,32,3,128]{3,2,1,0:T(4,128)S(1)} fusion(f32[8,32,3,128]{3,2,1,0:T(4,128)S(1)} %get-tuple-element.123, s32[]{:T(128)} %get-tuple-element.121, f32[32,128,128]{2,1,0:T(8,128)S(1)} %multiply_reduce_fusion.2, f32[32,128]{1,0:T(8,128)S(1)} %bitcast.59, f32[32,128]{1,0:T(8,128)S(1)} %dynamic-slice_bitcast_fusion.11, ...), kind=kOutput, calls=%fused_computation.8.clone.1 | convolution fusion | flops 20471808 | bytes 2360320 | tf_op jit(solution)/shard_map/while/body/eval_jaxpr/vmap()/dot_general | solution.py:15
  63.3 2.9 %fusion.18 = f32[8,32,3,128]{3,2,1,0:T(4,128)S(1)} fusion(f32[8,32,3,128]{3,2,1,0:T(4,128)S(1)} %get-tuple-element.122, s32[]{:T(128)} %get-tuple-element.121, f32[32,128,128]{2,1,0:T(8,128)S(1)} %multiply_reduce_fusion.2, f32[32,128]{1,0:T(8,128)S(1)} %bitcast.60, f32[32,128]{1,0:T(8,128)S(1)} %dynamic-slice_bitcast_fusion.11, ...), kind=kOutput, calls=%fused_computation.11.clone.1 | convolution fusion | flops 20471808 | bytes 2359300 | tf_op jit(solution)/shard_map/while/body/eval_jaxpr/vmap()/dot_general | solution.py:14
  66.3 2.1 multiply_reduce_fusion.2
  68.4 1.9 fusion.17
  70.3 4.2 %fusion.19 = f32[8,32,3,128]{3,2,1,0:T(4,128)S(1)} fusion(f32[8,32,3,128]{3,2,1,0:T(4,128)S(1)} %get-tuple-element.123, s32[]{:T(128)} %get-tuple-element.121, f32[32,128,128]{2,1,0:T(8,128)S(1)} %multiply_reduce_fusion.2, f32[32,128]{1,0:T(8,128)S(1)} %bitcast.59, f32[32,128]{1,0:T(8,128)S(1)} %dynamic-slice_bitcast_fusion.11, ...), kind=kOutput, calls=%fused_computation.8.clone.1 | convolution fusion | flops 20471808 | bytes 2360320 | tf_op jit(solution)/shard_map/while/body/eval_jaxpr/vmap()/dot_general | solution.py:15
  74.6 2.9 %fusion.18 = f32[8,32,3,128]{3,2,1,0:T(4,128)S(1)} fusion(f32[8,32,3,128]{3,2,1,0:T(4,128)S(1)} %get-tuple-element.122, s32[]{:T(128)} %get-tuple-element.121, f32[32,128,128]{2,1,0:T(8,128)S(1)} %multiply_reduce_fusion.2, f32[32,128]{1,0:T(8,128)S(1)} %bitcast.60, f32[32,128]{1,0:T(8,128)S(1)} %dynamic-slice_bitcast_fusion.11, ...), kind=kOutput, calls=%fused_computation.11.clone.1 | convolution fusion | flops 20471808 | bytes 2359300 | tf_op jit(solution)/shard_map/while/body/eval_jaxpr/vmap()/dot_general | solution.py:14
  77.6 2.1 multiply_reduce_fusion.2
  79.7 1.9 fusion.17
  81.6 4.2 %fusion.19 = f32[8,32,3,128]{3,2,1,0:T(4,128)S(1)} fusion(f32[8,32,3,128]{3,2,1,0:T(4,128)S(1)} %get-tuple-element.123, s32[]{:T(128)} %get-tuple-element.121, f32[32,128,128]{2,1,0:T(8,128)S(1)} %multiply_reduce_fusion.2, f32[32,128]{1,0:T(8,128)S(1)} %bitcast.59, f32[32,128]{1,0:T(8,128)S(1)} %dynamic-slice_bitcast_fusion.11, ...), kind=kOutput, calls=%fused_computation.8.clone.1 | convolution fusion | flops 20471808 | bytes 2360320 | tf_op jit(solution)/shard_map/while/body/eval_jaxpr/vmap()/dot_general | solution.py:15
  85.8 2.9 %fusion.18 = f32[8,32,3,128]{3,2,1,0:T(4,128)S(1)} fusion(f32[8,32,3,128]{3,2,1,0:T(4,128)S(1)} %get-tuple-element.122, s32[]{:T(128)} %get-tuple-element.121, f32[32,128,128]{2,1,0:T(8,128)S(1)} %multiply_reduce_fusion.2, f32[32,128]{1,0:T(8,128)S(1)} %bitcast.60, f32[32,128]{1,0:T(8,128)S(1)} %dynamic-slice_bitcast_fusion.11, ...), kind=kOutput, calls=%fused_computation.11.clone.1 | convolution fusion | flops 20471808 | bytes 2359300 | tf_op jit(solution)/shard_map/while/body/eval_jaxpr/vmap()/dot_general | solution.py:14
  88.8 2.1 multiply_reduce_fusion.2
  90.9 1.9 fusion.17
  92.8 4.2 %fusion.19 = f32[8,32,3,128]{3,2,1,0:T(4,128)S(1)} fusion(f32[8,32,3,128]{3,2,1,0:T(4,128)S(1)} %get-tuple-element.123, s32[]{:T(128)} %get-tuple-element.121, f32[32,128,128]{2,1,0:T(8,128)S(1)} %multiply_reduce_fusion.2, f32[32,128]{1,0:T(8,128)S(1)} %bitcast.59, f32[32,128]{1,0:T(8,128)S(1)} %dynamic-slice_bitcast_fusion.11, ...), kind=kOutput, calls=%fused_computation.8.clone.1 | convolution fusion | flops 20471808 | bytes 2360320 | tf_op jit(solution)/shard_map/while/body/eval_jaxpr/vmap()/dot_general | solution.py:15
  97.1 2.9 %fusion.18 = f32[8,32,3,128]{3,2,1,0:T(4,128)S(1)} fusion(f32[8,32,3,128]{3,2,1,0:T(4,128)S(1)} %get-tuple-element.122, s32[]{:T(128)} %get-tuple-element.121, f32[32,128,128]{2,1,0:T(8,128)S(1)} %multiply_reduce_fusion.2, f32[32,128]{1,0:T(8,128)S(1)} %bitcast.60, f32[32,128]{1,0:T(8,128)S(1)} %dynamic-slice_bitcast_fusion.11, ...), kind=kOutput, calls=%fused_computation.11.clone.1 | convolution fusion | flops 20471808 | bytes 2359300 | tf_op jit(solution)/shard_map/while/body/eval_jaxpr/vmap()/dot_general | solution.py:14
  100.0 2.1 multiply_reduce_fusion.2
  102.2 1.9 fusion.17
  104.1 4.2 %fusion.19 = f32[8,32,3,128]{3,2,1,0:T(4,128)S(1)} fusion(f32[8,32,3,128]{3,2,1,0:T(4,128)S(1)} %get-tuple-element.123, s32[]{:T(128)} %get-tuple-element.121, f32[32,128,128]{2,1,0:T(8,128)S(1)} %multiply_reduce_fusion.2, f32[32,128]{1,0:T(8,128)S(1)} %bitcast.59, f32[32,128]{1,0:T(8,128)S(1)} %dynamic-slice_bitcast_fusion.11, ...), kind=kOutput, calls=%fused_computation.8.clone.1 | convolution fusion | flops 20471808 | bytes 2360320 | tf_op jit(solution)/shard_map/while/body/eval_jaxpr/vmap()/dot_general | solution.py:15
  108.3 2.9 %fusion.18 = f32[8,32,3,128]{3,2,1,0:T(4,128)S(1)} fusion(f32[8,32,3,128]{3,2,1,0:T(4,128)S(1)} %get-tuple-element.122, s32[]{:T(128)} %get-tuple-element.121, f32[32,128,128]{2,1,0:T(8,128)S(1)} %multiply_reduce_fusion.2, f32[32,128]{1,0:T(8,128)S(1)} %bitcast.60, f32[32,128]{1,0:T(8,128)S(1)} %dynamic-slice_bitcast_fusion.11, ...), kind=kOutput, calls=%fused_computation.11.clone.1 | convolution fusion | flops 20471808 | bytes 2359300 | tf_op jit(solution)/shard_map/while/body/eval_jaxpr/vmap()/dot_general | solution.py:14
  111.3 2.1 multiply_reduce_fusion.2
  113.4 1.9 fusion.17
  115.3 4.2 %fusion.19 = f32[8,32,3,128]{3,2,1,0:T(4,128)S(1)} fusion(f32[8,32,3,128]{3,2,1,0:T(4,128)S(1)} %get-tuple-element.123, s32[]{:T(128)} %get-tuple-element.121, f32[32,128,128]{2,1,0:T(8,128)S(1)} %multiply_reduce_fusion.2, f32[32,128]{1,0:T(8,128)S(1)} %bitcast.59, f32[32,128]{1,0:T(8,128)S(1)} %dynamic-slice_bitcast_fusion.11, ...), kind=kOutput, calls=%fused_computation.8.clone.1 | convolution fusion | flops 20471808 | bytes 2360320 | tf_op jit(solution)/shard_map/while/body/eval_jaxpr/vmap()/dot_general | solution.py:15
  119.6 2.9 %fusion.18 = f32[8,32,3,128]{3,2,1,0:T(4,128)S(1)} fusion(f32[8,32,3,128]{3,2,1,0:T(4,128)S(1)} %get-tuple-element.122, s32[]{:T(128)} %get-tuple-element.121, f32[32,128,128]{2,1,0:T(8,128)S(1)} %multiply_reduce_fusion.2, f32[32,128]{1,0:T(8,128)S(1)} %bitcast.60, f32[32,128]{1,0:T(8,128)S(1)} %dynamic-slice_bitcast_fusion.11, ...), kind=kOutput, calls=%fused_computation.11.clone.1 | convolution fusion | flops 20471808 | bytes 2359300 | tf_op jit(solution)/shard_map/while/body/eval_jaxpr/vmap()/dot_general | solution.py:14
  122.5 2.1 multiply_reduce_fusion.2
  124.7 1.9 fusion.17
  126.6 4.2 %fusion.19 = f32[8,32,3,128]{3,2,1,0:T(4,128)S(1)} fusion(f32[8,32,3,128]{3,2,1,0:T(4,128)S(1)} %get-tuple-element.123, s32[]{:T(128)} %get-tuple-element.121, f32[32,128,128]{2,1,0:T(8,128)S(1)} %multiply_reduce_fusion.2, f32[32,128]{1,0:T(8,128)S(1)} %bitcast.59, f32[32,128]{1,0:T(8,128)S(1)} %dynamic-slice_bitcast_fusion.11, ...), kind=kOutput, calls=%fused_computation.8.clone.1 | convolution fusion | flops 20471808 | bytes 2360320 | tf_op jit(solution)/shard_map/while/body/eval_jaxpr/vmap()/dot_general | solution.py:15
  130.8 2.9 %fusion.18 = f32[8,32,3,128]{3,2,1,0:T(4,128)S(1)} fusion(f32[8,32,3,128]{3,2,1,0:T(4,128)S(1)} %get-tuple-element.122, s32[]{:T(128)} %get-tuple-element.121, f32[32,128,128]{2,1,0:T(8,128)S(1)} %multiply_reduce_fusion.2, f32[32,128]{1,0:T(8,128)S(1)} %bitcast.60, f32[32,128]{1,0:T(8,128)S(1)} %dynamic-slice_bitcast_fusion.11, ...), kind=kOutput, calls=%fused_computation.11.clone.1 | convolution fusion | flops 20471808 | bytes 2359300 | tf_op jit(solution)/shard_map/while/body/eval_jaxpr/vmap()/dot_general | solution.py:14
  133.7 0.0 copy-start.6
  133.7 0.1 broadcast_in_dim.39
  133.8 8.4 %scatter_fusion = f32[256,3,128]{2,1,0:T(4,128)S(1)} fusion(f32[256,3,128]{2,1,0:T(4,128)S(1)} %broadcast_in_dim.39, s32[256]{0:T(256)S(1)} %bitcast.73, f32[256,3,128]{2,1,0:T(4,128)S(1)} %bitcast.65), kind=kCustom, calls=%fused_computation.3 | custom fusion | flops 98304 | bytes 1180672 | tf_op jit(solution)/shard_map/scatter-add | solution.py:64
  142.2 0.0 copy-start
  142.2 0.8 copy-done
  143.0 0.0 all-reduce.6.cloned.1.call-update
  143.0 0.0 all-reduce.4.cloned.1.call-start
  143.0 0.0 copy-done.6
  143.1 0.6 dynamic-slice
  144.3 38.5 %all-reduce.6.cloned.1.call-done = f32[256,3,128]{2,1,0:T(4,128)} async-done(((f32[256,3,128]{2,1,0:T(4,128)}), f32[256,3,128]{2,1,0:T(4,128)}) %all-reduce.6.cloned.1.call-update) | async-done | bytes 393232
  182.8 0.9 constant_dynamic-slice_fusion
  183.7 0.6 copy.39
  184.3 0.0 all-reduce.4.cloned.1.call-update
  184.4 0.1 reduce_sum.36
  184.4 8.3 %psum.15 = f32[16,3,128]{2,1,0:T(4,128)S(1)} all-reduce(f32[16,3,128]{2,1,0:T(4,128)S(1)} %reduce_sum.36), channel_id=1, replica_groups=mesh['groups'=2,'pair'=4,'mm'=2,'sub'=2] {'mm'}, use_global_device_ids=true, to_apply=%region_9.10 | all-reduce | flops 6144 | bytes 49152 | tf_op jit(solution)/shard_map/psum | solution.py:71
  192.8 0.6 copy.37
  193.4 10.1 %all-reduce.4.cloned.1.call-done = f32[64,1,3,128]{3,0,2,1:T(8,128)} async-done(((f32[64,1,3,128]{3,0,2,1:T(8,128)}), f32[64,1,3,128]{3,0,2,1:T(8,128)}) %all-reduce.4.cloned.1.call-update) | async-done | bytes 98320 | tf_op jit(solution)/shard_map/psum | solution.py:70
  203.5 1.6 copy.36
  (60 shorter events, 0.8 us)
Async XLA Ops:
  7.2 35.2 %copy-start.1 = (f32[16,3,128]{2,0,1:T(8,128)S(1)}, f32[16,3,128]{2,0,1:T(8,128)}, u32[]{:S(2)}) copy-start(f32[16,3,128]{2,0,1:T(8,128)} %param.10) | copy-start | bytes 73732
  7.2 35.3 %copy-start.5 = (s32[16]{0:T(128)S(1)}, s32[16]{0:T(128)}, u32[]{:S(2)}) copy-start(s32[16]{0:T(128)} %param.14) | copy-start | bytes 196
  7.2 35.4 %copy-start.3 = (f32[16,128]{1,0:T(8,128)S(1)}, f32[16,128]{1,0:T(8,128)}, u32[]{:S(2)}) copy-start(f32[16,128]{1,0:T(8,128)} %param.12) | copy-start | bytes 24580
  7.2 35.4 %copy-start.4 = (f32[16,128]{1,0:T(8,128)S(1)}, f32[16,128]{1,0:T(8,128)}, u32[]{:S(2)}) copy-start(f32[16,128]{1,0:T(8,128)} %param.13) | copy-start | bytes 24580
  7.2 35.5 %copy-start.2 = (f32[16,128]{1,0:T(8,128)S(1)}, f32[16,128]{1,0:T(8,128)}, u32[]{:S(2)}) copy-start(f32[16,128]{1,0:T(8,128)} %param.11) | copy-start | bytes 24580
  7.2 175.5 %all-reduce.6.cloned.1.call-start = ((), (), s32[]{:S(2)}) async-start(), calls=%async_computation.1 | async-start | bytes 1048576
  133.7 9.3 %copy-start.6 = (u32[32]{0:T(128)S(1)}, u32[32]{0:T(128)}, u32[]{:S(2)}) copy-start(u32[32]{0:T(128)} %constant.37) | copy-start | bytes 388
  142.2 0.8 copy-start
  143.0 60.5 %all-reduce.4.cloned.1.call-start = ((), (), s32[]{:S(2)}) async-start(), calls=%async_computation | async-start | bytes 196608 | tf_op jit(solution)/shard_map/psum | solution.py:70
Sparse Core Ops, SparseCore 0:
  143.1 39.5 all-reduce.5
  185.6 17.7 all-reduce.3
where the time goes:
time: 212 us
  matrix products  57 us (27%)
  waiting for transfers between devices  48.6 us (23%)
  other arithmetic  41.6 us (20%)
  blocking collectives  38.6 us (18%)
  between operations  14.9 us (7%)
  local copies, waits for them, and re-layouts  10.6 us (5%)
    unnamed x3, waiting for transfers between devices  38.5 us
    dot_general x8, matrix products, interact(): cross_pairs = jnp.dot(coords, coef.T, precision=lax.Precision.HIGHEST)  33.9 us
    dot_general x8, matrix products, interact(): cross_atoms = jnp.dot(centers, coef, precision=lax.Precision.HIGHEST)  23.1 us
    reduce_sum x8, other arithmetic, interact(): delta_sq = jnp.sum((coords[:, None, :] - centers[:, :, None]) ** 2, axis=0)  16.6 us
    all_gather x1, blocking collectives, body(): lax.all_gather(coords_here, 'pair', axis=0, tiled=True)  16.2 us
    reduce_sum x8, other arithmetic, interact(): row_total = jnp.sum(coef, axis=1)  15 us
    all_gather x1, blocking collectives, body(): lax.all_gather(charges_here, 'pair', axis=0, tiled=True)  14 us
    psum x1, waiting for transfers between devices, body(): mm_force = lax.psum(mm_part, 'sub')[:, None]  10.1 us
  transfers between devices with their start and end apart: 2, of which 2 were waited for; matrix products, arithmetic and copies ran while one was open for 1% of the time, Pallas kernels for 0%

commit v1 on v0

v1 whole, which is shorter than its diff:
```python
import functools

import jax
import jax.numpy as jnp
from jax import lax
from jax.experimental import pallas as pl
from jax.experimental.pallas import tpu as pltpu
from jax.sharding import PartitionSpec as P

ROWS = 16


def pair_kernel(
    pattern_ref, padding_ref, pkg_ref, atoms_ref, mm_ref, tile_ref, cols, near_atoms, acc, tsum
):
    tiles, _, pairs = pkg_ref.shape
    near = pattern_ref.shape[0] // tiles
    mm_ref[...] = jnp.zeros_like(mm_ref)

    def one_tile(t, carry):
        cols[:, 0:8] = pkg_ref[t].T
        tsum[...] = jnp.zeros_like(tsum)
        for n in range(near):
            b = pattern_ref[t * near + n]
            for i in range(4):
                near_atoms[n, i] = jnp.broadcast_to(atoms_ref[b, i : i + 1, :], (8, 128))
            for i in range(3):
                acc[n, i] = jnp.zeros((8, 128), jnp.float32)
        steps = (pairs - padding_ref[t] + ROWS - 1) // ROWS

        def one_step(j, carry):
            row = pl.multiple_of(j * ROWS, ROWS)
            groups = []
            for h in range(ROWS // 8):
                col = cols[pl.ds(row + 8 * h, 8), :]
                groups.append(
                    [jnp.broadcast_to(col[:, i : i + 1], (8, 128)) for i in range(5)]
                )
            total = [[None] * 3 for _ in groups]
            for n in range(near):
                x, y, z, q = (near_atoms[n, i] for i in range(4))
                here = [None] * 3
                for h, (cx, cy, cz, wid, wgt) in enumerate(groups):
                    dx, dy, dz = x - cx, y - cy, z - cz
                    s = (dx * dx + dy * dy) + (dz * dz + wid)
                    r = lax.rsqrt(s)
                    coef = (wgt * q) * (r * r * r)
                    for i, d in enumerate((dx, dy, dz)):
                        f = coef * d
                        here[i] = f if here[i] is None else here[i] + f
                        total[h][i] = f if total[h][i] is None else total[h][i] + f
                for i in range(3):
                    acc[n, i] += here[i]
            for h in range(len(groups)):
                for i in range(3):
                    tsum[pl.ds(row + 8 * h, 8), i : i + 1] = -jnp.sum(
                        total[h][i], axis=1, keepdims=True
                    )
            return carry

        lax.fori_loop(0, steps, one_step, 0)
        tile_ref[t] = tsum[:, 0:8].T
        for n in range(near):
            b = pattern_ref[t * near + n]
            rows = [jnp.sum(acc[n, i], axis=0, keepdims=True) for i in range(3)]
            for i in range(3):
                mm_ref[b, i : i + 1, :] += rows[i]
        return carry

    lax.fori_loop(0, tiles, one_tile, 0)


def interactions(blocks, padding, package, atoms):
    tiles, _, pairs = package.shape
    near = blocks.shape[0] // tiles
    vmem = pl.BlockSpec(memory_space=pltpu.VMEM)
    smem = pl.BlockSpec(memory_space=pltpu.SMEM)
    return pl.pallas_call(
        pair_kernel,
        out_shape=(
            jax.ShapeDtypeStruct((atoms.shape[0], 3, atoms.shape[2]), jnp.float32),
            jax.ShapeDtypeStruct((tiles, 8, pairs), jnp.float32),
        ),
        in_specs=[smem, smem, vmem, vmem],
        out_specs=(vmem, vmem),
        scratch_shapes=[
            pltpu.VMEM((pairs, 128), jnp.float32),
            pltpu.VMEM((near, 4, 8, 128), jnp.float32),
            pltpu.VMEM((near, 3, 8, 128), jnp.float32),
            pltpu.VMEM((pairs, 128), jnp.float32),
        ],
        compiler_params=pltpu.CompilerParams(vmem_limit_bytes=48 * 1024 * 1024),
    )(blocks, padding, package, atoms)


def body(centers, widths, density, prefactor, padding, pattern, mm_coords, mm_charges):
    pairs = centers.shape[2]
    slots = jnp.arange(pairs, dtype=jnp.int32)[None, :]
    weight = jnp.where(slots < (pairs - padding)[:, None], density * prefactor, jnp.float32(0.0))
    package = jnp.concatenate(
        [centers, widths[:, None, :], weight[:, None, :], jnp.zeros_like(centers)], axis=1
    )
    blocks = pattern[:, 0, :].reshape(-1)
    atoms = jnp.concatenate([mm_coords[:, 0], mm_charges], axis=1)
    atoms = lax.all_gather(atoms, "pair", axis=0, tiled=True)
    mm_part, tile_part = interactions(blocks, padding, package, atoms)
    mm_part = lax.psum_scatter(mm_part, "pair", scatter_dimension=0, tiled=True)
    mm_force = lax.psum(mm_part, "sub")[:, None]
    tile_force = lax.psum(tile_part[:, 0:3], "mm")
    return (mm_force, tile_force)


def solution(mesh):
    tiles = P(("groups", "pair", "sub"))
    placed = (
        tiles,
        tiles,
        tiles,
        tiles,
        tiles,
        P(("groups", "pair", "sub"), "mm", None),
        P(("groups", "pair"), "mm", None, None),
        P(("groups", "pair"), "mm", None),
    )
    return jax.shard_map(
        body,
        mesh=mesh,
        in_specs=placed,
        out_specs=(P(("groups", "pair"), "mm", None, None), tiles),
        check_vma=False,
    )
```

time: 212 us -> 130 us (0.61)
  matrix products: 57 us -> 0 us
  other arithmetic: 41.6 us -> 0.85 us
  Pallas kernels: 0 us -> 31 us
  blocking collectives: 38.6 us -> 25.7 us
    dot_general x16 -> x0, matrix products: 57 us -> none  [the longest x8 33.9 us: interact(): cross_pairs = jnp.dot(coords, coef.T, precision=lax.Precision.HIGHEST)]
    reduce_sum x17 -> x0, other arithmetic: 31.7 us -> none  [the longest x8 16.6 us: interact(): delta_sq = jnp.sum((coords[:, None, :] - centers[:, :, None]) ** 2, axis=0)]
    pallas_call x0 -> x1, Pallas kernels: none -> 31 us  [interactions(): pl.pallas_call(pair_kernel, out_shape=(jax.ShapeDtypeStruct((atoms.shape[...]
    all_gather x2 -> x1, blocking collectives: 30.2 us -> 17.4 us  [body(): atoms = lax.all_gather(atoms, 'pair', axis=0, tiled=True)]
    scatter-add x1 -> x0, other arithmetic: 8.35 us -> none  [body(): mm_part = lax.psum_scatter(jnp.zeros((owned * lax.axis_size('pair'), 3, a...]
    gather x3 -> x0, local copies, waits for them, and re-layouts: 2.75 us -> none  [the longest x1 1.03 us: body(): package[tile_of]]
    unnamed x21 -> x22, local copies, waits for them, and re-layouts: 6.02 us -> 6.72 us
where the time goes in v1:
time: 130 us; the launch traced here: 129 us
  waiting for transfers between devices  48.3 us (37%)
  Pallas kernels  31 us (24%)
  blocking collectives  25.7 us (20%)
  between operations  14.8 us (11%)
  local copies, waits for them, and re-layouts  8.54 us (7%)
    unnamed x3, waiting for transfers between devices  38.6 us
    pallas_call x1, Pallas kernels, interactions(): pl.pallas_call(pair_kernel, out_shape=(jax.ShapeDtypeStruct((atoms.shape[...  31 us
    all_gather x1, blocking collectives, body(): atoms = lax.all_gather(atoms, 'pair', axis=0, tiled=True)  17.4 us
    psum x1, waiting for transfers between devices, body(): mm_force = lax.psum(mm_part, 'sub')[:, None]  9.69 us
    psum x1, blocking collectives, body(): tile_force = lax.psum(tile_part[:, 0:3], 'mm')  8.33 us
    unnamed x22, local copies, waits for them, and re-layouts  6.72 us
  transfers between devices with their start and end apart: 2, of which 2 were waited for; matrix products, arithmetic and copies ran while one was open for 1% of the time, Pallas kernels for 0%

profile of v1, /device:TPU:0, one launch (start us, length us, event | category | flops | bytes accessed | tf_op | source)
XLA Modules:
  0.0 129.2 jit_solution(17972302725616083683)
XLA Ops:
  7.2 0.0 copy-start.1
  7.2 0.0 all-reduce.6.cloned.1.call-start
  7.2 0.9 copy.25
  8.1 0.0 copy-done.1
  8.1 0.1 copy.21
  8.2 0.0 copy-start.2
  8.3 17.4 %all_gather.3.atoms_ref = f32[256,4,128]{2,1,0:T(4,128)S(1)} all-gather(f32[64,4,128]{2,1,0:T(4,128)S(1)} %copy.21), channel_id=1, replica_groups=mesh['groups'=2,'pair'=4,'mm'=2,'sub'=2] {'pair'}, dimensions={0}, use_global_device_ids=true | all-gather | bytes 655360 | tf_op jit(solution)/shard_map/all_gather | solution.py:105
  25.6 0.0 copy-done.2
  25.6 0.0 copy-start
  25.6 0.0 copy-start.6
  25.6 0.6 copy-done
  26.3 0.5 broadcast.11
  26.8 0.0 copy-done.6
  26.8 0.0 copy-start.5
  26.8 0.7 reduce.3
  27.5 0.0 copy-start.4
  27.5 0.1 reshape_squeeze.3.pattern_ref
  27.6 0.1 pad.5.clone
  27.6 0.0 copy-done.5
  27.7 0.5 copy-done.4
  28.2 0.0 copy-start.3
  28.2 0.1 multiply_select_fusion
  28.3 0.6 copy-done.3
  28.9 0.1 maximum_maximum_fusion.pkg_ref
  29.0 31.0 %shard_map.95 = (f32[256,3,128]{2,1,0:T(4,128)}, f32[16,8,128]{2,1,0:T(8,128)S(1)}) custom-call(s32[256]{0:T(256)S(1)} %reshape_squeeze.3.pattern_ref, s32[16]{0:T(128)S(1)} %copy-done, f32[16,8,128]{2,1,0:T(8,128)S(1)} %maximum_maximum_fusion.pkg_ref, f32[256,4,128]{2,1,0:T(4,128)S(1)} %all_gather.3.atoms_ref), custom_call_target="tpu_custom_call" | custom-call | tf_op jit(solution)/shard_map/pallas_call | solution.py:78
  60.0 0.0 all-reduce.6.cloned.1.call-update
  60.0 0.0 all-reduce.4.cloned.1.call-start
  60.1 0.0 copy-start.7
  60.1 0.6 copy-done.7
  60.7 0.6 dynamic-slice
  62.0 38.5 %all-reduce.6.cloned.1.call-done = f32[256,3,128]{2,1,0:T(4,128)} async-done(((f32[256,3,128]{2,1,0:T(4,128)}), f32[256,3,128]{2,1,0:T(4,128)}) %all-reduce.6.cloned.1.call-update) | async-done | bytes 393232
  100.5 1.6 %dynamic-slice_bitcast_fusion = f32[64,1,3,128]{3,2,0,1:T(4,128)} fusion(f32[256,3,128]{2,1,0:T(4,128)} %all-reduce.6.cloned.1.call-done, u32[]{:T(128)S(6)} %multiply.1), kind=kLoop, calls=%fused_computation.1 | loop fusion | bytes 196612 | tf_op jit(solution)/shard_map/broadcast_in_dim | solution.py:108
  102.1 0.0 all-reduce.4.cloned.1.call-update
  102.1 8.3 %psum.15 = f32[16,3,128]{2,1,0:T(4,128)S(1)} all-reduce(f32[16,3,128]{2,1,0:T(4,128)S(1)} %slice.3), channel_id=1, replica_groups=mesh['groups'=2,'pair'=4,'mm'=2,'sub'=2] {'mm'}, use_global_device_ids=true, to_apply=%region_2.3 | all-reduce | flops 6144 | bytes 49152 | tf_op jit(solution)/shard_map/psum | solution.py:109
  110.4 0.6 copy.23
  111.0 9.7 %all-reduce.4.cloned.1.call-done = f32[64,1,3,128]{3,2,0,1:T(4,128)} async-done(((f32[64,1,3,128]{3,2,0,1:T(4,128)}), f32[64,1,3,128]{3,2,0,1:T(4,128)}) %all-reduce.4.cloned.1.call-update) | async-done | bytes 98320 | tf_op jit(solution)/shard_map/psum | solution.py:108
  120.7 1.6 %copy.22 = f32[64,1,3,128]{3,1,2,0:T(1,128)} copy(f32[64,1,3,128]{3,2,0,1:T(4,128)} %all-reduce.4.cloned.1.call-done) | data formatting | bytes 196608
  (5 shorter events, 0.0 us)
Async XLA Ops:
  7.2 1.0 copy-start.1
  7.2 93.3 %all-reduce.6.cloned.1.call-start = ((), (), s32[]{:S(2)}) async-start(), calls=%async_computation.1 | async-start | bytes 1048576
  8.2 17.4 %copy-start.2 = (f32[16,3,128]{2,0,1:T(8,128)S(1)}, f32[16,3,128]{2,0,1:T(8,128)}, u32[]{:S(2)}) copy-start(f32[16,3,128]{2,0,1:T(8,128)} %param.8) | copy-start | bytes 73732
  25.6 0.7 copy-start
  25.6 1.2 copy-start.6
  26.8 0.9 copy-start.5
  27.5 0.7 copy-start.4
  28.2 0.7 copy-start.3
  60.0 60.7 %all-reduce.4.cloned.1.call-start = ((), (), s32[]{:S(2)}) async-start(), calls=%async_computation | async-start | bytes 262144 | tf_op jit(solution)/shard_map/psum | solution.py:108
  60.1 0.7 copy-start.7
Sparse Core Ops, SparseCore 0:
  60.1 40.3 all-reduce.5
  102.8 17.8 all-reduce.3

commit v2 on v1

v2 whole, which is shorter than its diff:
```python
import functools

import jax
import jax.numpy as jnp
from jax import lax
from jax.experimental import pallas as pl
from jax.experimental.pallas import tpu as pltpu
from jax.sharding import PartitionSpec as P

ROWS = 16
LIMIT = 48 * 1024 * 1024
VMEM = pl.BlockSpec(memory_space=pltpu.VMEM)
SMEM = pl.BlockSpec(memory_space=pltpu.SMEM)


def remote(src, dst, send, recv, **where):
    return pltpu.make_async_remote_copy(
        src_ref=src,
        dst_ref=dst,
        send_sem=send,
        recv_sem=recv,
        device_id=where,
        device_id_type=pl.DeviceIdType.MESH,
    )


def greet(peers):
    barrier = pltpu.get_barrier_semaphore()
    for where in peers:
        pl.semaphore_signal(
            barrier, inc=1, device_id=where, device_id_type=pl.DeviceIdType.MESH
        )
    pl.semaphore_wait(barrier, len(peers))


def gather_kernel(n, coords_ref, charges_ref, out_ref, send, recv, core_send, core_recv):
    owned = coords_ref.shape[0]
    half = owned // 2
    p, s = lax.axis_index("pair"), lax.axis_index("sub")
    mine = pl.multiple_of(p * owned, owned)
    out_ref[pl.ds(mine, owned), 0:3, :] = coords_ref[:, 0]
    out_ref[pl.ds(mine, owned), 3:4, :] = charges_ref[...]
    peers = [lax.rem(p + k, n) for k in range(1, n)]
    greet([{"pair": q} for q in peers] + [{"sub": 1 - s}])

    def part(q):
        return out_ref.at[pl.ds(pl.multiple_of(q * owned + s * half, half), half)]

    out = [
        remote(part(p), part(p), send.at[k], recv.at[k], pair=q) for k, q in enumerate(peers)
    ]
    for copy in out:
        copy.start()
    across = []
    for k in range(n - 1):
        out[k].wait_recv()
        q = lax.rem(p + n - 1 - k, n)
        copy = remote(part(q), part(q), core_send.at[k], core_recv.at[k], sub=1 - s)
        copy.start()
        across.append(copy)
    for copy in across:
        copy.wait()
    for copy in out:
        copy.wait_send()


def gather(n, coords, charges):
    owned, _, _, atoms = coords.shape
    return pl.pallas_call(
        functools.partial(gather_kernel, n),
        out_shape=jax.ShapeDtypeStruct((n * owned, 4, atoms), jnp.float32),
        in_specs=[VMEM] * 2,
        out_specs=VMEM,
        scratch_shapes=[pltpu.SemaphoreType.DMA((n - 1,))] * 4,
        compiler_params=pltpu.CompilerParams(
            collective_id=0, has_side_effects=True, vmem_limit_bytes=LIMIT
        ),
    )(coords, charges)


def reduce_kernel(
    n,
    groups,
    part_ref,
    tile_ref,
    mm_ref,
    sum_ref,
    swapped,
    summed,
    landed,
    tile_landed,
    core_send,
    core_recv,
    send,
    recv,
    tile_send,
    tile_recv,
    last_send,
    last_recv,
):
    p, m, s = (lax.axis_index(a) for a in ("pair", "mm", "sub"))
    peers = [lax.rem(p + k, n) for k in range(1, n)] + [p]
    others = [lax.rem(m + k, groups) for k in range(1, groups)]
    greet([{"pair": q} for q in peers[:-1]] + [{"sub": 1 - s}] + [{"mm": g} for g in others])
    across = [
        remote(part_ref.at[q, 1 - s], swapped.at[k], core_send.at[k], core_recv.at[k], sub=1 - s)
        for k, q in enumerate(peers)
    ]
    for copy in across:
        copy.start()
    tiles = [
        remote(tile_ref, tile_landed.at[k], tile_send.at[k], tile_recv.at[k], mm=g)
        for k, g in enumerate(others)
    ]
    for copy in tiles:
        copy.start()
    out = []
    for k, q in enumerate(peers):
        across[k].wait_recv()
        if k < n - 1:
            summed[k] = part_ref[q, s] + swapped[k]
            copy = remote(summed.at[k], landed.at[k], send.at[k], recv.at[k], pair=q)
            copy.start()
            out.append(copy)
        else:
            total = part_ref[q, s] + swapped[k]
    for k, copy in enumerate(out):
        copy.wait_recv()
        total = total + landed[k]
    mm_ref[s] = total
    last = remote(mm_ref.at[s], mm_ref.at[s], last_send.at[0], last_recv.at[0], sub=1 - s)
    last.start()
    tile_total = tile_ref[...]
    for k, copy in enumerate(tiles):
        copy.wait_recv()
        tile_total = tile_total + tile_landed[k]
    sum_ref[...] = tile_total
    last.wait()
    for copy in across + out + tiles:
        copy.wait_send()


def reduce(n, groups, mm_part, tile_part):
    piece = mm_part.shape[2:]
    dma = pltpu.SemaphoreType.DMA
    return pl.pallas_call(
        functools.partial(reduce_kernel, n, groups),
        out_shape=(
            jax.ShapeDtypeStruct((2,) + piece, jnp.float32),
            jax.ShapeDtypeStruct(tile_part.shape, jnp.float32),
        ),
        in_specs=[VMEM] * 2,
        out_specs=(VMEM, VMEM),
        scratch_shapes=[
            pltpu.VMEM((n,) + piece, jnp.float32),
            pltpu.VMEM((n - 1,) + piece, jnp.float32),
            pltpu.VMEM((n - 1,) + piece, jnp.float32),
            pltpu.VMEM((groups - 1,) + tile_part.shape, jnp.float32),
            dma((n,)),
            dma((n,)),
            dma((n - 1,)),
            dma((n - 1,)),
            dma((groups - 1,)),
            dma((groups - 1,)),
            dma((1,)),
            dma((1,)),
        ],
        compiler_params=pltpu.CompilerParams(
            collective_id=1, has_side_effects=True, vmem_limit_bytes=LIMIT
        ),
    )(mm_part, tile_part)


def pair_kernel(
    pattern_ref,
    padding_ref,
    centers_ref,
    widths_ref,
    density_ref,
    prefactor_ref,
    atoms_ref,
    mm_ref,
    tile_ref,
    rows_scr,
    cols,
    near_atoms,
    acc,
    tsum,
):
    tiles, _, pairs = centers_ref.shape
    near = pattern_ref.shape[2]
    half = mm_ref.shape[1]
    mm_ref[...] = jnp.zeros_like(mm_ref)
    rows_scr[...] = jnp.zeros_like(rows_scr)
    slots = lax.broadcasted_iota(jnp.int32, (1, pairs), 1)

    def one_tile(t, carry):
        valid = pairs - padding_ref[t]
        rows_scr[0:3, :] = centers_ref[t]
        rows_scr[3:4, :] = widths_ref[pl.ds(t, 1), :]
        rows_scr[4:5, :] = jnp.where(
            slots < valid, density_ref[pl.ds(t, 1), :] * prefactor_ref[pl.ds(t, 1), :], 0.0
        )
        cols[:, 0:8] = rows_scr[...].T
        tsum[...] = jnp.zeros_like(tsum)
        for n in range(near):
            b = pattern_ref[t, 0, n]
            for i in range(4):
                near_atoms[n, i] = jnp.broadcast_to(atoms_ref[b, i : i + 1, :], (8, 128))
            for i in range(3):
                acc[n, i] = jnp.zeros((8, 128), jnp.float32)
        steps = lax.div(valid + ROWS - 1, ROWS)

        def one_step(j, carry):
            row = pl.multiple_of(j * ROWS, ROWS)
            groups = []
            for h in range(ROWS // 8):
                col = cols[pl.ds(row + 8 * h, 8), :]
                groups.append(
                    [jnp.broadcast_to(col[:, i : i + 1], (8, 128)) for i in range(5)]
                )
            total = [[None] * 3 for _ in groups]
            for n in range(near):
                x, y, z, q = (near_atoms[n, i] for i in range(4))
                here = [None] * 3
                for h, (cx, cy, cz, wid, wgt) in enumerate(groups):
                    dx, dy, dz = x - cx, y - cy, z - cz
                    s = (dx * dx + dy * dy) + (dz * dz + wid)
                    r = lax.rsqrt(s)
                    coef = (wgt * q) * (r * r * r)
                    for i, d in enumerate((dx, dy, dz)):
                        f = coef * d
                        here[i] = f if here[i] is None else here[i] + f
                        total[h][i] = f if total[h][i] is None else total[h][i] + f
                for i in range(3):
                    acc[n, i] += here[i]
            for h in range(len(groups)):
                for i in range(3):
                    tsum[pl.ds(row + 8 * h, 8), i : i + 1] = -jnp.sum(
                        total[h][i], axis=1, keepdims=True
                    )
            return carry

        lax.fori_loop(0, steps, one_step, 0)
        forces = tsum[:, 0:8].T
        for i in range(3):
            tile_ref[i, pl.ds(t, 1), :] = forces[i : i + 1, :]
        for n in range(near):
            b = pattern_ref[t, 0, n]
            piece = lax.div(b, half)
            row = b - piece * half
            for i in range(3):
                mm_ref[piece * 3 + i, pl.ds(row, 1), :] += jnp.sum(
                    acc[n, i], axis=0, keepdims=True
                )
        return carry

    lax.fori_loop(0, tiles, one_tile, 0)


def interactions(half, pattern, padding, centers, widths, density, prefactor, atoms):
    tiles, _, pairs = centers.shape
    near = pattern.shape[2]
    return pl.pallas_call(
        pair_kernel,
        out_shape=(
            jax.ShapeDtypeStruct((atoms.shape[0] // half * 3, half, 128), jnp.float32),
            jax.ShapeDtypeStruct((3, tiles, pairs), jnp.float32),
        ),
        in_specs=[SMEM] * 2 + [VMEM] * 5,
        out_specs=(VMEM, VMEM),
        scratch_shapes=[
            pltpu.VMEM((8, pairs), jnp.float32),
            pltpu.VMEM((pairs, 128), jnp.float32),
            pltpu.VMEM((near, 4, 8, 128), jnp.float32),
            pltpu.VMEM((near, 3, 8, 128), jnp.float32),
            pltpu.VMEM((pairs, 128), jnp.float32),
        ],
        compiler_params=pltpu.CompilerParams(vmem_limit_bytes=LIMIT),
    )(pattern, padding, centers, widths, density, prefactor, atoms)


def body(n, groups, centers, widths, density, prefactor, padding, pattern, mm_coords, mm_charges):
    owned = mm_coords.shape[0]
    half = owned // 2
    atoms = gather(n, mm_coords, mm_charges)
    mm_part, tile_part = interactions(
        half, pattern, padding, centers, widths, density, prefactor, atoms
    )
    mm_part = mm_part.reshape(n, 2, 3, half, mm_coords.shape[3])
    mm_force, tile_force = reduce(n, groups, mm_part, tile_part)
    mm_force = mm_force.transpose(0, 2, 1, 3).reshape(mm_coords.shape)
    return (mm_force, tile_force.transpose(1, 0, 2))


def solution(mesh):
    tiles = P(("groups", "pair", "sub"))
    placed = (
        tiles,
        tiles,
        tiles,
        tiles,
        tiles,
        P(("groups", "pair", "sub"), "mm", None),
        P(("groups", "pair"), "mm", None, None),
        P(("groups", "pair"), "mm", None),
    )
    return jax.shard_map(
        functools.partial(body, mesh.shape["pair"], mesh.shape["mm"]),
        mesh=mesh,
        in_specs=placed,
        out_specs=(P(("groups", "pair"), "mm", None, None), tiles),
        check_vma=False,
    )
```

time: 130 us -> 56.7 us (0.44)
  waiting for transfers between devices: 48.3 us -> 0 us
  blocking collectives: 25.7 us -> 0 us
  Pallas kernels: 31 us -> 52.7 us
  between operations: 14.8 us -> 0.76 us
  local copies, waits for them, and re-layouts: 8.54 us -> 3.07 us
    unnamed x3 -> x0, waiting for transfers between devices: 38.6 us -> none
    pallas_call x0 -> x2, Pallas kernels: none -> 21.5 us  [the longest x1 12 us: gather(): pl.pallas_call(functools.partial(gather_kernel, n), out_shape=jax.ShapeDt...]
    all_gather x1 -> x0, blocking collectives: 17.4 us -> none  [body(): atoms = lax.all_gather(atoms, 'pair', axis=0, tiled=True)]
    psum x1 -> x0, waiting for transfers between devices: 9.69 us -> none  [body(): mm_force = lax.psum(mm_part, 'sub')[:, None]]
    psum x1 -> x0, blocking collectives: 8.33 us -> none  [body(): tile_force = lax.psum(tile_part[:, 0:3], 'mm')]
    unnamed x22 -> x16, local copies, waits for them, and re-layouts: 6.72 us -> 3.06 us
    broadcast_in_dim x2 -> x0, local copies, waits for them, and re-layouts: 1.57 us -> none  [the longest x1 1.57 us: body(): mm_force = lax.psum(mm_part, 'sub')[:, None]]
  transfers between devices with their start and end apart: 2 -> 0, of which waited for: 2 -> 0; matrix products, arithmetic and copies ran while one was open for 1% -> 0% of each run, Pallas kernels for 0% -> 0%
where the time goes in v2:
time: 56.7 us; the launch traced here: 56.5 us
  Pallas kernels  52.7 us (93%)
  local copies, waits for them, and re-layouts  3.07 us (5%)
  between operations  0.76 us (1%)
    pallas_call x1, Pallas kernels, interactions(): pl.pallas_call(pair_kernel, out_shape=(jax.ShapeDtypeStruct((atoms.shape[...  31.2 us
    pallas_call x1, Pallas kernels, gather(): pl.pallas_call(functools.partial(gather_kernel, n), out_shape=jax.ShapeDt...  12 us
    pallas_call x1, Pallas kernels, reduce(): pl.pallas_call(functools.partial(reduce_kernel, n, groups), out_shape=(ja...  9.56 us
    unnamed x16, local copies, waits for them, and re-layouts  3.06 us

profile of v2, /device:TPU:0, one launch (start us, length us, event | category | flops | bytes accessed | tf_op | source)
XLA Modules:
  0.0 56.5 jit_solution(16792601787358925846)
XLA Ops:
  0.6 0.8 %copy.13.centers_ref = f32[16,3,128]{2,1,0:T(4,128)S(1)} copy(f32[16,3,128]{2,0,1:T(8,128)} %param.8) | data formatting | bytes 49152 | tf_op args[0]
  1.4 0.0 copy-start
  1.4 0.9 %copy.12.coords_ref = f32[64,1,3,128]{3,2,1,0:T(4,128)S(1)} copy(f32[64,1,3,128]{3,1,2,0:T(1,128)} %param.14) | data formatting | bytes 196608 | tf_op args[6]
  2.3 0.0 copy-done
  2.3 0.0 copy-start.1
  2.3 0.0 copy-start.2
  2.4 0.0 copy-start.3
  2.4 0.0 copy-start.4
  2.4 0.0 copy-start.5
  2.4 12.0 %shard_map.95.atoms_ref = f32[256,4,128]{2,1,0:T(4,128)S(1)} custom-call(f32[64,1,3,128]{3,2,1,0:T(4,128)S(1)} %copy.12.coords_ref, f32[64,1,128]{2,1,0:T(1,128)S(1)} %copy-done), custom_call_target="tpu_custom_call" | custom-call | tf_op jit(solution)/shard_map/pallas_call | solution.py:69
  14.4 0.0 copy-done.1
  14.4 0.0 copy-done.2
  14.4 0.0 copy-done.3
  14.4 0.0 copy-done.4
  14.4 0.0 copy-done.5
  14.4 31.2 %shard_map.96 = (f32[24,32,128]{2,1,0:T(8,128)S(1)}, f32[3,16,128]{2,1,0:T(8,128)S(1)}) custom-call(s32[16,1,16]{2,1,0:T(1,128)S(1)} %copy-done.1, s32[16]{0:T(128)S(1)} %copy-done.5, f32[16,3,128]{2,1,0:T(4,128)S(1)} %copy.13.centers_ref, f32[16,128]{1,0:T(8,128)S(1)} %copy-done.2, f32[16,128]{1,0:T(8,128)S(1)} %copy-done.3, f32[16,128]{1,0:T(8,128)S(1)} %copy-done.4, ...), custom_call_target="tpu_custom_call" | custom-call | tf_op jit(solution)/shard_map/pallas_call | solution.py:264
  45.6 9.6 %shard_map.97 = (f32[2,3,32,128]{3,2,1,0:T(8,128)S(1)}, f32[3,16,128]{2,1,0:T(8,128)S(1)}) custom-call(f32[4,2,3,32,128]{4,3,2,1,0:T(8,128)S(1)} %bitcast.4, f32[3,16,128]{2,1,0:T(8,128)S(1)} %get-tuple-element.7.tile_ref), custom_call_target="tpu_custom_call" | custom-call | tf_op jit(solution)/shard_map/pallas_call | solution.py:146
  55.2 0.7 %copy.15 = f32[64,1,3,128]{3,1,2,0:T(1,128)} copy(f32[64,1,3,128]{3,0,2,1:T(8,128)S(1)} %bitcast.7) | data formatting | bytes 196608
  55.9 0.6 %copy.17 = f32[16,3,128]{2,0,1:T(8,128)} copy(f32[16,3,128]{2,0,1:T(8,128)S(1)} %bitcast.6) | data formatting | bytes 49152
  (1 shorter events, 0.0 us)
Async XLA Ops:
  1.4 0.9 %copy-start = (f32[64,1,128]{2,1,0:T(1,128)S(1)}, f32[64,1,128]{2,1,0:T(1,128)}, u32[]{:S(2)}) copy-start(f32[64,1,128]{2,1,0:T(1,128)} %charges_ref.1) | copy-start | bytes 98308
  2.3 12.0 %copy-start.1 = (s32[16,1,16]{2,1,0:T(1,128)S(1)}, s32[16,1,16]{2,1,0:T(1,128)}, u32[]{:S(2)}) copy-start(s32[16,1,16]{2,1,0:T(1,128)} %pattern_ref.1) | copy-start | bytes 3076
  2.3 12.0 %copy-start.2 = (f32[16,128]{1,0:T(8,128)S(1)}, f32[16,128]{1,0:T(8,128)}, u32[]{:S(2)}) copy-start(f32[16,128]{1,0:T(8,128)} %widths_ref.1) | copy-start | bytes 24580
  2.4 12.0 %copy-start.3 = (f32[16,128]{1,0:T(8,128)S(1)}, f32[16,128]{1,0:T(8,128)}, u32[]{:S(2)}) copy-start(f32[16,128]{1,0:T(8,128)} %density_ref.1) | copy-start | bytes 24580
  2.4 12.0 %copy-start.4 = (f32[16,128]{1,0:T(8,128)S(1)}, f32[16,128]{1,0:T(8,128)}, u32[]{:S(2)}) copy-start(f32[16,128]{1,0:T(8,128)} %prefactor_ref.1) | copy-start | bytes 24580
  2.4 12.0 %copy-start.5 = (s32[16]{0:T(128)S(1)}, s32[16]{0:T(128)}, u32[]{:S(2)}) copy-start(s32[16]{0:T(128)} %padding_ref.1) | copy-start | bytes 196

commit v3 on v2

--- a/solution.py
+++ b/solution.py
@@ -181,28 +181,46 @@
     atoms_ref,
     mm_ref,
     tile_ref,
-    rows_scr,
-    cols,
+    wide,
     near_atoms,
     acc,
-    tsum,
+    total,
 ):
     tiles, _, pairs = centers_ref.shape
     near = pattern_ref.shape[2]
     half = mm_ref.shape[1]
     mm_ref[...] = jnp.zeros_like(mm_ref)
-    rows_scr[...] = jnp.zeros_like(rows_scr)
     slots = lax.broadcasted_iota(jnp.int32, (1, pairs), 1)
+    part = lax.broadcasted_iota(jnp.int32, (32, 5 * 128), 0)
+    column = lax.broadcasted_iota(jnp.int32, (32, 5 * 128), 1)
+    spread = jnp.where(
+        (part < 24) & ((part & 7) == (column >> 7)), 1.0, 0.0
+    ).astype(jnp.bfloat16)
+    for t in range(tiles):
+        weight = jnp.where(
+            slots < pairs - padding_ref[t],
+            density_ref[t : t + 1, :] * prefactor_ref[t : t + 1, :],
+            0.0,
+        )
+        rest = jnp.concatenate(
+            [centers_ref[t], widths_ref[t : t + 1, :], weight, jnp.zeros((3, pairs), jnp.float32)],
+            axis=0,
+        )
+        pieces = []
+        for _ in range(3):
+            piece = rest.astype(jnp.bfloat16).astype(jnp.float32)
+            pieces.append(piece)
+            rest = rest - piece
+        pieces.append(jnp.zeros_like(rest))
+        pieces = jnp.concatenate(pieces, axis=0).astype(jnp.bfloat16)
+        over = lax.dot_general(
+            pieces, spread, (((0,), (0,)), ((), ())), preferred_element_type=jnp.float32
+        )
+        for i in range(5):
+            wide[t, i] = over[:, 128 * i : 128 * (i + 1)]
 
     def one_tile(t, carry):
         valid = pairs - padding_ref[t]
-        rows_scr[0:3, :] = centers_ref[t]
-        rows_scr[3:4, :] = widths_ref[pl.ds(t, 1), :]
-        rows_scr[4:5, :] = jnp.where(
-            slots < valid, density_ref[pl.ds(t, 1), :] * prefactor_ref[pl.ds(t, 1), :], 0.0
-        )
-        cols[:, 0:8] = rows_scr[...].T
-        tsum[...] = jnp.zeros_like(tsum)
         for n in range(near):
             b = pattern_ref[t, 0, n]
             for i in range(4):
@@ -213,13 +231,11 @@
 
         def one_step(j, carry):
             row = pl.multiple_of(j * ROWS, ROWS)
-            groups = []
-            for h in range(ROWS // 8):
-                col = cols[pl.ds(row + 8 * h, 8), :]
-                groups.append(
-                    [jnp.broadcast_to(col[:, i : i + 1], (8, 128)) for i in range(5)]
-                )
-            total = [[None] * 3 for _ in groups]
+            groups = [
+                [wide[t, i, pl.ds(row + 8 * h, 8), :] for i in range(5)]
+                for h in range(ROWS // 8)
+            ]
+            sums = [[None] * 3 for _ in groups]
             for n in range(near):
                 x, y, z, q = (near_atoms[n, i] for i in range(4))
                 here = [None] * 3
@@ -231,20 +247,15 @@
                     for i, d in enumerate((dx, dy, dz)):
                         f = coef * d
                         here[i] = f if here[i] is None else here[i] + f
-                        total[h][i] = f if total[h][i] is None else total[h][i] + f
+                        sums[h][i] = f if sums[h][i] is None else sums[h][i] + f
                 for i in range(3):
                     acc[n, i] += here[i]
             for h in range(len(groups)):
                 for i in range(3):
-                    tsum[pl.ds(row + 8 * h, 8), i : i + 1] = -jnp.sum(
-                        total[h][i], axis=1, keepdims=True
-                    )
+                    total[t, i, pl.ds(row + 8 * h, 8), :] = sums[h][i]
             return carry
 
         lax.fori_loop(0, steps, one_step, 0)
-        forces = tsum[:, 0:8].T
-        for i in range(3):
-            tile_ref[i, pl.ds(t, 1), :] = forces[i : i + 1, :]
         for n in range(near):
             b = pattern_ref[t, 0, n]
             piece = lax.div(b, half)
@@ -256,6 +267,21 @@
         return carry
 
     lax.fori_loop(0, tiles, one_tile, 0)
+    ones = jnp.ones((16, 2 * 128), jnp.bfloat16)
+    for t in range(tiles):
+        for i in range(3):
+            whole = total[t, i]
+            high = whole.astype(jnp.bfloat16)
+            low = (whole - high.astype(jnp.float32)).astype(jnp.bfloat16)
+            line = lax.dot_general(
+                ones,
+                jnp.concatenate([high, low], axis=1),
+                (((1,), (1,)), ((), ())),
+                preferred_element_type=jnp.float32,
+            )
+            tile_ref[i, t : t + 1, :] = jnp.where(
+                slots < pairs - padding_ref[t], -line[0:1, :], 0.0
+            )
 
 
 def interactions(half, pattern, padding, centers, widths, density, prefactor, atoms):
@@ -270,11 +296,10 @@
         in_specs=[SMEM] * 2 + [VMEM] * 5,
         out_specs=(VMEM, VMEM),
         scratch_shapes=[
-            pltpu.VMEM((8, pairs), jnp.float32),
-            pltpu.VMEM((pairs, 128), jnp.float32),
+            pltpu.VMEM((tiles, 5, pairs, 128), jnp.float32),
             pltpu.VMEM((near, 4, 8, 128), jnp.float32),
             pltpu.VMEM((near, 3, 8, 128), jnp.float32),
-            pltpu.VMEM((pairs, 128), jnp.float32),
+            pltpu.VMEM((tiles, 3, pairs, 128), jnp.float32),
         ],
         compiler_params=pltpu.CompilerParams(vmem_limit_bytes=LIMIT),
     )(pattern, padding, centers, widths, density, prefactor, atoms)

time: 56.7 us -> 41.8 us (0.74)
  Pallas kernels: 52.7 us -> 37.7 us
    pallas_call x1, Pallas kernels: 31.2 us -> 15.1 us  [interactions(): pl.pallas_call(pair_kernel, out_shape=(jax.ShapeDtypeStruct((atoms.shape[...]
    pallas_call x1, Pallas kernels: 9.56 us -> 10.6 us  [reduce(): pl.pallas_call(functools.partial(reduce_kernel, n, groups), out_shape=(ja...]
where the time goes in v3:
time: 41.8 us; the launch traced here: 41.5 us
  Pallas kernels  37.7 us (90%)
  local copies, waits for them, and re-layouts  3.07 us (7%)
  between operations  0.75 us (2%)
    pallas_call x1, Pallas kernels, interactions(): pl.pallas_call(pair_kernel, out_shape=(jax.ShapeDtypeStruct((atoms.shape[...  15.1 us
    pallas_call x1, Pallas kernels, gather(): pl.pallas_call(functools.partial(gather_kernel, n), out_shape=jax.ShapeDt...  12 us
    pallas_call x1, Pallas kernels, reduce(): pl.pallas_call(functools.partial(reduce_kernel, n, groups), out_shape=(ja...  10.6 us
    unnamed x16, local copies, waits for them, and re-layouts  3.06 us

profile of v3, /device:TPU:0, one launch (start us, length us, event | category | flops | bytes accessed | tf_op | source)
XLA Modules:
  0.0 41.5 jit_solution(3657113303681330596)
XLA Ops:
  0.6 0.8 %copy.13.centers_ref = f32[16,3,128]{2,1,0:T(4,128)S(1)} copy(f32[16,3,128]{2,0,1:T(8,128)} %param.8) | data formatting | bytes 49152 | tf_op args[0]
  1.4 0.0 copy-start
  1.4 0.9 %copy.12.coords_ref = f32[64,1,3,128]{3,2,1,0:T(4,128)S(1)} copy(f32[64,1,3,128]{3,1,2,0:T(1,128)} %param.14) | data formatting | bytes 196608 | tf_op args[6]
  2.3 0.0 copy-done
  2.3 0.0 copy-start.1
  2.3 0.0 copy-start.2
  2.4 0.0 copy-start.3
  2.4 0.0 copy-start.4
  2.4 0.0 copy-start.5
  2.4 12.0 %shard_map.95.atoms_ref = f32[256,4,128]{2,1,0:T(4,128)S(1)} custom-call(f32[64,1,3,128]{3,2,1,0:T(4,128)S(1)} %copy.12.coords_ref, f32[64,1,128]{2,1,0:T(1,128)S(1)} %copy-done), custom_call_target="tpu_custom_call" | custom-call | tf_op jit(solution)/shard_map/pallas_call | solution.py:69
  14.4 0.0 copy-done.1
  14.4 0.0 copy-done.2
  14.4 0.0 copy-done.3
  14.4 0.0 copy-done.4
  14.4 0.0 copy-done.5
  14.4 15.1 %shard_map.96 = (f32[24,32,128]{2,1,0:T(8,128)S(1)}, f32[3,16,128]{2,1,0:T(8,128)S(1)}) custom-call(s32[16,1,16]{2,1,0:T(1,128)S(1)} %copy-done.1, s32[16]{0:T(128)S(1)} %copy-done.5, f32[16,3,128]{2,1,0:T(4,128)S(1)} %copy.13.centers_ref, f32[16,128]{1,0:T(8,128)S(1)} %copy-done.2, f32[16,128]{1,0:T(8,128)S(1)} %copy-done.3, f32[16,128]{1,0:T(8,128)S(1)} %copy-done.4, ...), custom_call_target="tpu_custom_call" | custom-call | tf_op jit(solution)/shard_map/pallas_call | solution.py:290
  29.5 10.6 %shard_map.97 = (f32[2,3,32,128]{3,2,1,0:T(8,128)S(1)}, f32[3,16,128]{2,1,0:T(8,128)S(1)}) custom-call(f32[4,2,3,32,128]{4,3,2,1,0:T(8,128)S(1)} %bitcast.4, f32[3,16,128]{2,1,0:T(8,128)S(1)} %get-tuple-element.7.tile_ref), custom_call_target="tpu_custom_call" | custom-call | tf_op jit(solution)/shard_map/pallas_call | solution.py:146
  40.2 0.7 %copy.15 = f32[64,1,3,128]{3,1,2,0:T(1,128)} copy(f32[64,1,3,128]{3,0,2,1:T(8,128)S(1)} %bitcast.7) | data formatting | bytes 196608
  40.9 0.6 %copy.17 = f32[16,3,128]{2,0,1:T(8,128)} copy(f32[16,3,128]{2,0,1:T(8,128)S(1)} %bitcast.6) | data formatting | bytes 49152
  (1 shorter events, 0.0 us)
Async XLA Ops:
  1.4 0.9 %copy-start = (f32[64,1,128]{2,1,0:T(1,128)S(1)}, f32[64,1,128]{2,1,0:T(1,128)}, u32[]{:S(2)}) copy-start(f32[64,1,128]{2,1,0:T(1,128)} %charges_ref.1) | copy-start | bytes 98308
  2.3 12.0 %copy-start.1 = (s32[16,1,16]{2,1,0:T(1,128)S(1)}, s32[16,1,16]{2,1,0:T(1,128)}, u32[]{:S(2)}) copy-start(s32[16,1,16]{2,1,0:T(1,128)} %pattern_ref.1) | copy-start | bytes 3076
  2.3 12.0 %copy-start.2 = (f32[16,128]{1,0:T(8,128)S(1)}, f32[16,128]{1,0:T(8,128)}, u32[]{:S(2)}) copy-start(f32[16,128]{1,0:T(8,128)} %widths_ref.1) | copy-start | bytes 24580
  2.4 12.0 %copy-start.3 = (f32[16,128]{1,0:T(8,128)S(1)}, f32[16,128]{1,0:T(8,128)}, u32[]{:S(2)}) copy-start(f32[16,128]{1,0:T(8,128)} %density_ref.1) | copy-start | bytes 24580
  2.4 12.0 %copy-start.4 = (f32[16,128]{1,0:T(8,128)S(1)}, f32[16,128]{1,0:T(8,128)}, u32[]{:S(2)}) copy-start(f32[16,128]{1,0:T(8,128)} %prefactor_ref.1) | copy-start | bytes 24580
  2.4 12.0 %copy-start.5 = (s32[16]{0:T(128)S(1)}, s32[16]{0:T(128)}, u32[]{:S(2)}) copy-start(s32[16]{0:T(128)} %padding_ref.1) | copy-start | bytes 196

commit v4 on v3

--- a/solution.py
+++ b/solution.py
@@ -34,12 +34,13 @@
 
 
 def gather_kernel(n, coords_ref, charges_ref, out_ref, send, recv, core_send, core_recv):
-    owned = coords_ref.shape[0]
+    first = coords_ref.shape[0]
+    owned = first + charges_ref.shape[0]
     half = owned // 2
     p, s = lax.axis_index("pair"), lax.axis_index("sub")
     mine = pl.multiple_of(p * owned, owned)
-    out_ref[pl.ds(mine, owned), 0:3, :] = coords_ref[:, 0]
-    out_ref[pl.ds(mine, owned), 3:4, :] = charges_ref[...]
+    out_ref[pl.ds(mine, first), :] = coords_ref[...]
+    out_ref[pl.ds(mine + first, owned - first), :] = charges_ref[...]
     peers = [lax.rem(p + k, n) for k in range(1, n)]
     greet([{"pair": q} for q in peers] + [{"sub": 1 - s}])
 
@@ -65,10 +66,10 @@
 
 
 def gather(n, coords, charges):
-    owned, _, _, atoms = coords.shape
+    rows = coords.shape[0] + charges.shape[0]
     return pl.pallas_call(
         functools.partial(gather_kernel, n),
-        out_shape=jax.ShapeDtypeStruct((n * owned, 4, atoms), jnp.float32),
+        out_shape=jax.ShapeDtypeStruct((n * rows, coords.shape[1]), jnp.float32),
         in_specs=[VMEM] * 2,
         out_specs=VMEM,
         scratch_shapes=[pltpu.SemaphoreType.DMA((n - 1,))] * 4,
@@ -172,6 +173,7 @@
 
 
 def pair_kernel(
+    owned,
     pattern_ref,
     padding_ref,
     centers_ref,
@@ -186,9 +188,8 @@
     acc,
     total,
 ):
-    tiles, _, pairs = centers_ref.shape
+    _, tiles, pairs = centers_ref.shape
     near = pattern_ref.shape[2]
-    half = mm_ref.shape[1]
     mm_ref[...] = jnp.zeros_like(mm_ref)
     slots = lax.broadcasted_iota(jnp.int32, (1, pairs), 1)
     part = lax.broadcasted_iota(jnp.int32, (32, 5 * 128), 0)
@@ -203,7 +204,8 @@
             0.0,
         )
         rest = jnp.concatenate(
-            [centers_ref[t], widths_ref[t : t + 1, :], weight, jnp.zeros((3, pairs), jnp.float32)],
+            [centers_ref[i, t : t + 1, :] for i in range(3)]
+            + [widths_ref[t : t + 1, :], weight, jnp.zeros((3, pairs), jnp.float32)],
             axis=0,
         )
         pieces = []
@@ -223,8 +225,12 @@
         valid = pairs - padding_ref[t]
         for n in range(near):
             b = pattern_ref[t, 0, n]
-            for i in range(4):
-                near_atoms[n, i] = jnp.broadcast_to(atoms_ref[b, i : i + 1, :], (8, 128))
+            shard = lax.div(b, owned)
+            for i in range(3):
+                row = b * 3 + shard * owned + i
+                near_atoms[n, i] = jnp.broadcast_to(atoms_ref[pl.ds(row, 1), :], (8, 128))
+            row = b + (shard + 1) * (3 * owned)
+            near_atoms[n, 3] = jnp.broadcast_to(atoms_ref[pl.ds(row, 1), :], (8, 128))
             for i in range(3):
                 acc[n, i] = jnp.zeros((8, 128), jnp.float32)
         steps = lax.div(valid + ROWS - 1, ROWS)
@@ -258,12 +264,8 @@
         lax.fori_loop(0, steps, one_step, 0)
         for n in range(near):
             b = pattern_ref[t, 0, n]
-            piece = lax.div(b, half)
-            row = b - piece * half
             for i in range(3):
-                mm_ref[piece * 3 + i, pl.ds(row, 1), :] += jnp.sum(
-                    acc[n, i], axis=0, keepdims=True
-                )
+                mm_ref[pl.ds(b * 3 + i, 1), :] += jnp.sum(acc[n, i], axis=0, keepdims=True)
         return carry
 
     lax.fori_loop(0, tiles, one_tile, 0)
@@ -284,13 +286,13 @@
             )
 
 
-def interactions(half, pattern, padding, centers, widths, density, prefactor, atoms):
-    tiles, _, pairs = centers.shape
+def interactions(owned, pattern, padding, centers, widths, density, prefactor, atoms):
+    _, tiles, pairs = centers.shape
     near = pattern.shape[2]
     return pl.pallas_call(
-        pair_kernel,
+        functools.partial(pair_kernel, owned),
         out_shape=(
-            jax.ShapeDtypeStruct((atoms.shape[0] // half * 3, half, 128), jnp.float32),
+            jax.ShapeDtypeStruct((atoms.shape[0] // 4 * 3, 128), jnp.float32),
             jax.ShapeDtypeStruct((3, tiles, pairs), jnp.float32),
         ),
         in_specs=[SMEM] * 2 + [VMEM] * 5,
@@ -306,16 +308,21 @@
 
 
 def body(n, groups, centers, widths, density, prefactor, padding, pattern, mm_coords, mm_charges):
-    owned = mm_coords.shape[0]
-    half = owned // 2
-    atoms = gather(n, mm_coords, mm_charges)
+    owned, lanes = mm_coords.shape[0], mm_coords.shape[3]
+    atoms = gather(n, mm_coords.reshape(3 * owned, lanes), mm_charges.reshape(owned, lanes))
     mm_part, tile_part = interactions(
-        half, pattern, padding, centers, widths, density, prefactor, atoms
+        owned,
+        pattern,
+        padding,
+        centers.transpose(1, 0, 2),
+        widths,
+        density,
+        prefactor,
+        atoms,
     )
-    mm_part = mm_part.reshape(n, 2, 3, half, mm_coords.shape[3])
+    mm_part = mm_part.reshape(n, 2, 3 * owned // 2, lanes)
     mm_force, tile_force = reduce(n, groups, mm_part, tile_part)
-    mm_force = mm_force.transpose(0, 2, 1, 3).reshape(mm_coords.shape)
-    return (mm_force, tile_force.transpose(1, 0, 2))
+    return (mm_force.reshape(mm_coords.shape), tile_force.transpose(1, 0, 2))
 
 
 def solution(mesh):

time: 41.8 us -> 42.1 us (level)
  Pallas kernels: 37.7 us -> 38.3 us
    pallas_call x1, Pallas kernels: 15.1 us -> 16.4 us  [interactions(): pl.pallas_call(functools.partial(pair_kernel, owned), out_shape=(jax.Shap...]
    pallas_call x1, Pallas kernels: 10.6 us -> 9.96 us  [reduce(): pl.pallas_call(functools.partial(reduce_kernel, n, groups), out_shape=(ja...]
    unnamed x16 -> x18, local copies, waits for them, and re-layouts: 3.06 us -> 2.92 us
where the time goes in v4:
time: 42.1 us; the launch traced here: 41.9 us
  Pallas kernels  38.3 us (91%)
  local copies, waits for them, and re-layouts  2.92 us (7%)
  between operations  0.73 us (2%)
    pallas_call x1, Pallas kernels, interactions(): pl.pallas_call(functools.partial(pair_kernel, owned), out_shape=(jax.Shap...  16.4 us
    pallas_call x1, Pallas kernels, gather(): pl.pallas_call(functools.partial(gather_kernel, n), out_shape=jax.ShapeDt...  11.9 us
    pallas_call x1, Pallas kernels, reduce(): pl.pallas_call(functools.partial(reduce_kernel, n, groups), out_shape=(ja...  9.96 us
    unnamed x18, local copies, waits for them, and re-layouts  2.92 us

profile of v4, /device:TPU:0, one launch (start us, length us, event | category | flops | bytes accessed | tf_op | source)
XLA Modules:
  0.0 41.9 jit_solution(18017483086850807901)
XLA Ops:
  0.6 0.0 copy-start
  0.6 0.9 %copy-done = f32[64,1,3,128]{3,1,2,0:T(1,128)S(1)} copy-done((f32[64,1,3,128]{3,1,2,0:T(1,128)S(1)}, f32[64,1,3,128]{3,1,2,0:T(1,128)}, u32[]{:S(2)}) %copy-start) | copy-done | bytes 98328
  1.5 0.0 copy-start.1
  1.5 0.8 %copy-done.1 = f32[64,1,128]{2,1,0:T(1,128)S(1)} copy-done((f32[64,1,128]{2,1,0:T(1,128)S(1)}, f32[64,1,128]{2,1,0:T(1,128)}, u32[]{:S(2)}) %copy-start.1) | copy-done | bytes 32792
  2.3 0.0 copy-start.2
  2.3 0.0 copy-start.3
  2.3 0.0 copy-start.4
  2.3 0.0 copy-start.5
  2.3 0.0 copy-start.6
  2.3 0.0 copy-start.7
  2.3 11.9 %shard_map.95.atoms_ref = f32[1024,128]{1,0:T(8,128)S(1)} custom-call(f32[192,128]{1,0:T(8,128)S(1)} %bitcast.7, f32[64,128]{1,0:T(8,128)S(1)} %bitcast.9), custom_call_target="tpu_custom_call" | custom-call | tf_op jit(solution)/shard_map/pallas_call | solution.py:70
  14.3 0.0 copy-done.2
  14.3 0.0 copy-done.3
  14.3 0.0 copy-done.4
  14.3 0.0 copy-done.5
  14.3 0.0 copy-done.6
  14.3 0.0 copy-done.7
  14.3 16.4 %shard_map.96 = (f32[768,128]{1,0:T(8,128)S(1)}, f32[3,16,128]{2,1,0:T(8,128)S(1)}) custom-call(s32[16,1,16]{2,1,0:T(1,128)S(1)} %copy-done.3, s32[16]{0:T(128)S(1)} %copy-done.7, f32[3,16,128]{2,1,0:T(8,128)S(1)} %bitcast.11, f32[16,128]{1,0:T(8,128)S(1)} %copy-done.4, f32[16,128]{1,0:T(8,128)S(1)} %copy-done.5, f32[16,128]{1,0:T(8,128)S(1)} %copy-done.6, ...), custom_call_target="tpu_custom_call" | custom-call | tf_op jit(solution)/shard_map/pallas_call | solution.py:292
  30.7 10.0 %shard_map.97 = (f32[2,96,128]{2,1,0:T(8,128)S(1)}, f32[3,16,128]{2,1,0:T(8,128)S(1)}) custom-call(f32[4,2,96,128]{3,2,1,0:T(8,128)S(1)} %bitcast.6, f32[3,16,128]{2,1,0:T(8,128)S(1)} %get-tuple-element.7.tile_ref), custom_call_target="tpu_custom_call" | custom-call | tf_op jit(solution)/shard_map/pallas_call | solution.py:147
  40.7 0.6 %copy.14 = f32[64,1,3,128]{3,1,2,0:T(1,128)} copy(f32[64,1,3,128]{3,1,2,0:T(1,128)S(1)} %bitcast.8) | data formatting | bytes 196608
  41.3 0.6 %copy.15 = f32[16,3,128]{2,0,1:T(8,128)} copy(f32[16,3,128]{2,0,1:T(8,128)S(1)} %bitcast.10) | data formatting | bytes 49152
Async XLA Ops:
  0.6 0.9 %copy-start = (f32[64,1,3,128]{3,1,2,0:T(1,128)S(1)}, f32[64,1,3,128]{3,1,2,0:T(1,128)}, u32[]{:S(2)}) copy-start(f32[64,1,3,128]{3,1,2,0:T(1,128)} %param.14) | copy-start | bytes 294916
  1.5 0.8 %copy-start.1 = (f32[64,1,128]{2,1,0:T(1,128)S(1)}, f32[64,1,128]{2,1,0:T(1,128)}, u32[]{:S(2)}) copy-start(f32[64,1,128]{2,1,0:T(1,128)} %param.15) | copy-start | bytes 98308
  2.3 12.0 %copy-start.2 = (f32[16,3,128]{2,0,1:T(8,128)S(1)}, f32[16,3,128]{2,0,1:T(8,128)}, u32[]{:S(2)}) copy-start(f32[16,3,128]{2,0,1:T(8,128)} %param.8) | copy-start | bytes 73732
  2.3 12.0 %copy-start.3 = (s32[16,1,16]{2,1,0:T(1,128)S(1)}, s32[16,1,16]{2,1,0:T(1,128)}, u32[]{:S(2)}) copy-start(s32[16,1,16]{2,1,0:T(1,128)} %pattern_ref.1) | copy-start | bytes 3076
  2.3 12.0 %copy-start.4 = (f32[16,128]{1,0:T(8,128)S(1)}, f32[16,128]{1,0:T(8,128)}, u32[]{:S(2)}) copy-start(f32[16,128]{1,0:T(8,128)} %widths_ref.1) | copy-start | bytes 24580
  2.3 12.0 %copy-start.5 = (f32[16,128]{1,0:T(8,128)S(1)}, f32[16,128]{1,0:T(8,128)}, u32[]{:S(2)}) copy-start(f32[16,128]{1,0:T(8,128)} %density_ref.1) | copy-start | bytes 24580
  2.3 12.0 %copy-start.6 = (f32[16,128]{1,0:T(8,128)S(1)}, f32[16,128]{1,0:T(8,128)}, u32[]{:S(2)}) copy-start(f32[16,128]{1,0:T(8,128)} %prefactor_ref.1) | copy-start | bytes 24580
  2.3 12.0 %copy-start.7 = (s32[16]{0:T(128)S(1)}, s32[16]{0:T(128)}, u32[]{:S(2)}) copy-start(s32[16]{0:T(128)} %padding_ref.1) | copy-start | bytes 196

commit v5 on v4

--- a/solution.py
+++ b/solution.py
@@ -8,7 +8,7 @@
 from jax.sharding import PartitionSpec as P
 
 ROWS = 16
-LIMIT = 48 * 1024 * 1024
+LIMIT = 24 * 1024 * 1024
 VMEM = pl.BlockSpec(memory_space=pltpu.VMEM)
 SMEM = pl.BlockSpec(memory_space=pltpu.SMEM)
 
@@ -33,14 +33,10 @@
     pl.semaphore_wait(barrier, len(peers))
 
 
-def gather_kernel(n, coords_ref, charges_ref, out_ref, send, recv, core_send, core_recv):
-    first = coords_ref.shape[0]
-    owned = first + charges_ref.shape[0]
+def gather_kernel(n, shard_ref, out_ref, send, recv, core_send, core_recv):
+    owned = shard_ref.shape[0]
     half = owned // 2
     p, s = lax.axis_index("pair"), lax.axis_index("sub")
-    mine = pl.multiple_of(p * owned, owned)
-    out_ref[pl.ds(mine, first), :] = coords_ref[...]
-    out_ref[pl.ds(mine + first, owned - first), :] = charges_ref[...]
     peers = [lax.rem(p + k, n) for k in range(1, n)]
     greet([{"pair": q} for q in peers] + [{"sub": 1 - s}])
 
@@ -48,10 +44,18 @@
         return out_ref.at[pl.ds(pl.multiple_of(q * owned + s * half, half), half)]
 
     out = [
-        remote(part(p), part(p), send.at[k], recv.at[k], pair=q) for k, q in enumerate(peers)
+        remote(
+            shard_ref.at[pl.ds(pl.multiple_of(s * half, half), half)],
+            part(p),
+            send.at[k],
+            recv.at[k],
+            pair=q,
+        )
+        for k, q in enumerate(peers)
     ]
     for copy in out:
         copy.start()
+    out_ref[pl.ds(pl.multiple_of(p * owned, owned), owned), :] = shard_ref[...]
     across = []
     for k in range(n - 1):
         out[k].wait_recv()
@@ -65,18 +69,17 @@
         copy.wait_send()
 
 
-def gather(n, coords, charges):
-    rows = coords.shape[0] + charges.shape[0]
+def gather(n, shard):
     return pl.pallas_call(
         functools.partial(gather_kernel, n),
-        out_shape=jax.ShapeDtypeStruct((n * rows, coords.shape[1]), jnp.float32),
-        in_specs=[VMEM] * 2,
+        out_shape=jax.ShapeDtypeStruct((n * shard.shape[0], shard.shape[1]), jnp.float32),
+        in_specs=[VMEM],
         out_specs=VMEM,
         scratch_shapes=[pltpu.SemaphoreType.DMA((n - 1,))] * 4,
         compiler_params=pltpu.CompilerParams(
             collective_id=0, has_side_effects=True, vmem_limit_bytes=LIMIT
         ),
-    )(coords, charges)
+    )(shard)
 
 
 def reduce_kernel(
@@ -309,7 +312,10 @@
 
 def body(n, groups, centers, widths, density, prefactor, padding, pattern, mm_coords, mm_charges):
     owned, lanes = mm_coords.shape[0], mm_coords.shape[3]
-    atoms = gather(n, mm_coords.reshape(3 * owned, lanes), mm_charges.reshape(owned, lanes))
+    shard = jnp.concatenate(
+        [mm_coords.reshape(3 * owned, lanes), mm_charges.reshape(owned, lanes)], axis=0
+    )
+    atoms = gather(n, shard)
     mm_part, tile_part = interactions(
         owned,
         pattern,

time: 42.1 us -> 41.4 us (0.983); the launches traced: 41.9 us -> 41.7 us
  local copies, waits for them, and re-layouts: 2.92 us -> 1.29 us
  other arithmetic: 0 us -> 0.92 us
  Pallas kernels: 38.3 us -> 38.8 us
    unnamed x18 -> x14, local copies, waits for them, and re-layouts: 2.92 us -> 1.29 us
    pallas_call x1, Pallas kernels: 9.96 us -> 11.5 us  [reduce(): pl.pallas_call(functools.partial(reduce_kernel, n, groups), out_shape=(ja...]
    pallas_call x1, Pallas kernels: 16.4 us -> 15.3 us  [interactions(): pl.pallas_call(functools.partial(pair_kernel, owned), out_shape=(jax.Shap...]
    concatenate x0 -> x1, other arithmetic: none -> 0.92 us  [body(): jnp.concatenate([mm_coords.reshape(3 * owned, lanes), mm_charges.reshape(...]
where the time goes in v5:
time: 41.4 us; the launch traced here: 41.7 us
  Pallas kernels  38.8 us (94%)
  local copies, waits for them, and re-layouts  1.29 us (3%)
  other arithmetic  0.92 us (2%)
  between operations  0.74 us (2%)
    pallas_call x1, Pallas kernels, interactions(): pl.pallas_call(functools.partial(pair_kernel, owned), out_shape=(jax.Shap...  15.3 us
    pallas_call x1, Pallas kernels, gather(): pl.pallas_call(functools.partial(gather_kernel, n), out_shape=jax.ShapeDt...  11.9 us
    pallas_call x1, Pallas kernels, reduce(): pl.pallas_call(functools.partial(reduce_kernel, n, groups), out_shape=(ja...  11.5 us
    unnamed x14, local copies, waits for them, and re-layouts  1.29 us
    concatenate x1, other arithmetic, body(): jnp.concatenate([mm_coords.reshape(3 * owned, lanes), mm_charges.reshape(...  0.92 us

profile of v5, /device:TPU:0, one launch (start us, length us, event | category | flops | bytes accessed | tf_op | source)
XLA Modules:
  0.0 41.7 jit_solution(145080609235381230)
XLA Ops:
  0.6 0.9 %pad_maximum_fusion.shard_ref = f32[256,128]{1,0:T(8,128)S(1)} fusion(f32[64,128]{1,0:T(8,128)} %bitcast.11, f32[192,128]{1,0:T(8,128)} %bitcast.10), kind=kLoop, calls=%fused_computation | loop fusion | flops 32768 | bytes 262144 | tf_op jit(solution)/shard_map/concatenate | solution.py:315
  1.6 0.0 copy-start
  1.6 0.0 copy-start.1
  1.6 0.0 copy-start.2
  1.6 0.0 copy-start.3
  1.6 0.0 copy-start.4
  1.6 0.0 copy-start.5
  1.6 11.9 %shard_map.95.atoms_ref = f32[1024,128]{1,0:T(8,128)S(1)} custom-call(f32[256,128]{1,0:T(8,128)S(1)} %pad_maximum_fusion.shard_ref), custom_call_target="tpu_custom_call" | custom-call | tf_op jit(solution)/shard_map/pallas_call | solution.py:73
  13.6 0.0 copy-done
  13.6 0.0 copy-done.1
  13.6 0.0 copy-done.2
  13.6 0.0 copy-done.3
  13.6 0.0 copy-done.4
  13.6 0.0 copy-done.5
  13.6 15.3 %shard_map.96 = (f32[768,128]{1,0:T(8,128)S(1)}, f32[3,16,128]{2,1,0:T(8,128)S(1)}) custom-call(s32[16,1,16]{2,1,0:T(1,128)S(1)} %copy-done.1, s32[16]{0:T(128)S(1)} %copy-done.5, f32[3,16,128]{2,1,0:T(8,128)S(1)} %bitcast.9, f32[16,128]{1,0:T(8,128)S(1)} %copy-done.2, f32[16,128]{1,0:T(8,128)S(1)} %copy-done.3, f32[16,128]{1,0:T(8,128)S(1)} %copy-done.4, ...), custom_call_target="tpu_custom_call" | custom-call | tf_op jit(solution)/shard_map/pallas_call | solution.py:295
  29.0 11.5 %shard_map.97 = (f32[2,96,128]{2,1,0:T(8,128)S(1)}, f32[3,16,128]{2,1,0:T(8,128)S(1)}) custom-call(f32[4,2,96,128]{3,2,1,0:T(8,128)S(1)} %bitcast.6, f32[3,16,128]{2,1,0:T(8,128)S(1)} %get-tuple-element.7.tile_ref), custom_call_target="tpu_custom_call" | custom-call | tf_op jit(solution)/shard_map/pallas_call | solution.py:150
  40.5 0.6 %copy.14 = f32[64,1,3,128]{3,1,2,0:T(1,128)} copy(f32[64,1,3,128]{3,1,2,0:T(1,128)S(1)} %bitcast.7) | data formatting | bytes 196608
  41.1 0.6 %copy.15 = f32[16,3,128]{2,0,1:T(8,128)} copy(f32[16,3,128]{2,0,1:T(8,128)S(1)} %bitcast.8) | data formatting | bytes 49152
Async XLA Ops:
  1.6 12.0 %copy-start = (f32[16,3,128]{2,0,1:T(8,128)S(1)}, f32[16,3,128]{2,0,1:T(8,128)}, u32[]{:S(2)}) copy-start(f32[16,3,128]{2,0,1:T(8,128)} %param.8) | copy-start | bytes 73732
  1.6 12.0 %copy-start.1 = (s32[16,1,16]{2,1,0:T(1,128)S(1)}, s32[16,1,16]{2,1,0:T(1,128)}, u32[]{:S(2)}) copy-start(s32[16,1,16]{2,1,0:T(1,128)} %pattern_ref.1) | copy-start | bytes 3076
  1.6 12.0 %copy-start.2 = (f32[16,128]{1,0:T(8,128)S(1)}, f32[16,128]{1,0:T(8,128)}, u32[]{:S(2)}) copy-start(f32[16,128]{1,0:T(8,128)} %widths_ref.1) | copy-start | bytes 24580
  1.6 12.0 %copy-start.3 = (f32[16,128]{1,0:T(8,128)S(1)}, f32[16,128]{1,0:T(8,128)}, u32[]{:S(2)}) copy-start(f32[16,128]{1,0:T(8,128)} %density_ref.1) | copy-start | bytes 24580
  1.6 12.0 %copy-start.4 = (f32[16,128]{1,0:T(8,128)S(1)}, f32[16,128]{1,0:T(8,128)}, u32[]{:S(2)}) copy-start(f32[16,128]{1,0:T(8,128)} %prefactor_ref.1) | copy-start | bytes 24580
  1.6 12.0 %copy-start.5 = (s32[16]{0:T(128)S(1)}, s32[16]{0:T(128)}, u32[]{:S(2)}) copy-start(s32[16]{0:T(128)} %padding_ref.1) | copy-start | bytes 196

commit v6 on v3

--- a/solution.py
+++ b/solution.py
@@ -8,7 +8,7 @@
 from jax.sharding import PartitionSpec as P
 
 ROWS = 16
-LIMIT = 48 * 1024 * 1024
+LIMIT = 24 * 1024 * 1024
 VMEM = pl.BlockSpec(memory_space=pltpu.VMEM)
 SMEM = pl.BlockSpec(memory_space=pltpu.SMEM)
 
@@ -33,13 +33,10 @@
     pl.semaphore_wait(barrier, len(peers))
 
 
-def gather_kernel(n, coords_ref, charges_ref, out_ref, send, recv, core_send, core_recv):
-    owned = coords_ref.shape[0]
+def gather_kernel(n, shard_ref, out_ref, send, recv, core_send, core_recv):
+    owned = shard_ref.shape[0]
     half = owned // 2
     p, s = lax.axis_index("pair"), lax.axis_index("sub")
-    mine = pl.multiple_of(p * owned, owned)
-    out_ref[pl.ds(mine, owned), 0:3, :] = coords_ref[:, 0]
-    out_ref[pl.ds(mine, owned), 3:4, :] = charges_ref[...]
     peers = [lax.rem(p + k, n) for k in range(1, n)]
     greet([{"pair": q} for q in peers] + [{"sub": 1 - s}])
 
@@ -47,10 +44,18 @@
         return out_ref.at[pl.ds(pl.multiple_of(q * owned + s * half, half), half)]
 
     out = [
-        remote(part(p), part(p), send.at[k], recv.at[k], pair=q) for k, q in enumerate(peers)
+        remote(
+            shard_ref.at[pl.ds(pl.multiple_of(s * half, half), half)],
+            part(p),
+            send.at[k],
+            recv.at[k],
+            pair=q,
+        )
+        for k, q in enumerate(peers)
     ]
     for copy in out:
         copy.start()
+    out_ref[pl.ds(pl.multiple_of(p * owned, owned), owned)] = shard_ref[...]
     across = []
     for k in range(n - 1):
         out[k].wait_recv()
@@ -64,18 +69,17 @@
         copy.wait_send()
 
 
-def gather(n, coords, charges):
-    owned, _, _, atoms = coords.shape
+def gather(n, shard):
     return pl.pallas_call(
         functools.partial(gather_kernel, n),
-        out_shape=jax.ShapeDtypeStruct((n * owned, 4, atoms), jnp.float32),
-        in_specs=[VMEM] * 2,
+        out_shape=jax.ShapeDtypeStruct((n * shard.shape[0],) + shard.shape[1:], jnp.float32),
+        in_specs=[VMEM],
         out_specs=VMEM,
         scratch_shapes=[pltpu.SemaphoreType.DMA((n - 1,))] * 4,
         compiler_params=pltpu.CompilerParams(
             collective_id=0, has_side_effects=True, vmem_limit_bytes=LIMIT
         ),
-    )(coords, charges)
+    )(shard)
 
 
 def reduce_kernel(
@@ -186,7 +190,7 @@
     acc,
     total,
 ):
-    tiles, _, pairs = centers_ref.shape
+    _, tiles, pairs = centers_ref.shape
     near = pattern_ref.shape[2]
     half = mm_ref.shape[1]
     mm_ref[...] = jnp.zeros_like(mm_ref)
@@ -203,7 +207,8 @@
             0.0,
         )
         rest = jnp.concatenate(
-            [centers_ref[t], widths_ref[t : t + 1, :], weight, jnp.zeros((3, pairs), jnp.float32)],
+            [centers_ref[i, t : t + 1, :] for i in range(3)]
+            + [widths_ref[t : t + 1, :], weight, jnp.zeros((3, pairs), jnp.float32)],
             axis=0,
         )
         pieces = []
@@ -285,7 +290,7 @@
 
 
 def interactions(half, pattern, padding, centers, widths, density, prefactor, atoms):
-    tiles, _, pairs = centers.shape
+    _, tiles, pairs = centers.shape
     near = pattern.shape[2]
     return pl.pallas_call(
         pair_kernel,
@@ -308,9 +313,9 @@
 def body(n, groups, centers, widths, density, prefactor, padding, pattern, mm_coords, mm_charges):
     owned = mm_coords.shape[0]
     half = owned // 2
-    atoms = gather(n, mm_coords, mm_charges)
+    atoms = gather(n, jnp.concatenate([mm_coords[:, 0], mm_charges], axis=1))
     mm_part, tile_part = interactions(
-        half, pattern, padding, centers, widths, density, prefactor, atoms
+        half, pattern, padding, centers.transpose(1, 0, 2), widths, density, prefactor, atoms
     )
     mm_part = mm_part.reshape(n, 2, 3, half, mm_coords.shape[3])
     mm_force, tile_force = reduce(n, groups, mm_part, tile_part)

time: 41.8 us -> 41.8 us (level)
    unnamed x16 -> x17, local copies, waits for them, and re-layouts: 3.06 us -> 2.97 us
where the time goes in v6:
time: 41.8 us; the launch traced here: 41.7 us
  Pallas kernels  37.8 us (90%)
  local copies, waits for them, and re-layouts  3.04 us (7%)
  between operations  0.76 us (2%)
    pallas_call x1, Pallas kernels, interactions(): pl.pallas_call(pair_kernel, out_shape=(jax.ShapeDtypeStruct((atoms.shape[...  15.1 us
    pallas_call x1, Pallas kernels, gather(): pl.pallas_call(functools.partial(gather_kernel, n), out_shape=jax.ShapeDt...  11.9 us
    pallas_call x1, Pallas kernels, reduce(): pl.pallas_call(functools.partial(reduce_kernel, n, groups), out_shape=(ja...  10.7 us
    unnamed x17, local copies, waits for them, and re-layouts  2.97 us

profile of v6, /device:TPU:0, one launch (start us, length us, event | category | flops | bytes accessed | tf_op | source)
XLA Modules:
  0.0 41.7 jit_solution(14723660202808724124)
XLA Ops:
  0.6 0.9 %copy.15 = f32[64,1,3,128]{3,0,2,1:T(8,128)S(1)} copy(f32[64,1,3,128]{3,1,2,0:T(1,128)} %param.14) | data formatting | bytes 196608 | tf_op args[6]
  1.5 0.0 copy-start.6
  1.5 0.1 copy.11
  1.6 0.7 %copy-done.6 = f32[64,1,128]{2,1,0:T(1,128)S(1)} copy-done((f32[64,1,128]{2,1,0:T(1,128)S(1)}, f32[64,1,128]{2,1,0:T(1,128)}, u32[]{:S(2)}) %copy-start.6) | copy-done | bytes 32792
  2.3 0.1 pad_maximum_fusion.shard_ref
  2.4 0.0 copy-start
  2.4 0.0 copy-start.1
  2.4 0.0 copy-start.2
  2.4 0.0 copy-start.3
  2.4 0.0 copy-start.4
  2.4 0.0 copy-start.5
  2.4 11.9 %shard_map.95.atoms_ref = f32[256,4,128]{2,1,0:T(4,128)S(1)} custom-call(f32[64,4,128]{2,1,0:T(4,128)S(1)} %pad_maximum_fusion.shard_ref), custom_call_target="tpu_custom_call" | custom-call | tf_op jit(solution)/shard_map/pallas_call | solution.py:73
  14.4 0.0 copy-done
  14.4 0.0 copy-done.1
  14.4 0.0 copy-done.2
  14.4 0.0 copy-done.3
  14.4 0.0 copy-done.4
  14.4 0.0 copy-done.5
  14.4 15.1 %shard_map.96 = (f32[24,32,128]{2,1,0:T(8,128)S(1)}, f32[3,16,128]{2,1,0:T(8,128)S(1)}) custom-call(s32[16,1,16]{2,1,0:T(1,128)S(1)} %copy-done.1, s32[16]{0:T(128)S(1)} %copy-done.5, f32[3,16,128]{2,1,0:T(8,128)S(1)} %bitcast.11, f32[16,128]{1,0:T(8,128)S(1)} %copy-done.2, f32[16,128]{1,0:T(8,128)S(1)} %copy-done.3, f32[16,128]{1,0:T(8,128)S(1)} %copy-done.4, ...), custom_call_target="tpu_custom_call" | custom-call | tf_op jit(solution)/shard_map/pallas_call | solution.py:295
  29.6 10.7 %shard_map.97 = (f32[2,3,32,128]{3,2,1,0:T(8,128)S(1)}, f32[3,16,128]{2,1,0:T(8,128)S(1)}) custom-call(f32[4,2,3,32,128]{4,3,2,1,0:T(8,128)S(1)} %bitcast.8, f32[3,16,128]{2,1,0:T(8,128)S(1)} %get-tuple-element.7.tile_ref), custom_call_target="tpu_custom_call" | custom-call | tf_op jit(solution)/shard_map/pallas_call | solution.py:150
  40.3 0.7 %copy.13 = f32[64,1,3,128]{3,1,2,0:T(1,128)} copy(f32[64,1,3,128]{3,0,2,1:T(8,128)S(1)} %bitcast.12) | data formatting | bytes 196608
  41.1 0.6 %copy.17 = f32[16,3,128]{2,0,1:T(8,128)} copy(f32[16,3,128]{2,0,1:T(8,128)S(1)} %bitcast.10) | data formatting | bytes 49152
  (1 shorter events, 0.0 us)
Async XLA Ops:
  1.5 0.8 %copy-start.6 = (f32[64,1,128]{2,1,0:T(1,128)S(1)}, f32[64,1,128]{2,1,0:T(1,128)}, u32[]{:S(2)}) copy-start(f32[64,1,128]{2,1,0:T(1,128)} %param.15) | copy-start | bytes 98308
  2.4 12.0 %copy-start = (f32[16,3,128]{2,0,1:T(8,128)S(1)}, f32[16,3,128]{2,0,1:T(8,128)}, u32[]{:S(2)}) copy-start(f32[16,3,128]{2,0,1:T(8,128)} %param.8) | copy-start | bytes 73732
  2.4 12.0 %copy-start.1 = (s32[16,1,16]{2,1,0:T(1,128)S(1)}, s32[16,1,16]{2,1,0:T(1,128)}, u32[]{:S(2)}) copy-start(s32[16,1,16]{2,1,0:T(1,128)} %pattern_ref.1) | copy-start | bytes 3076
  2.4 12.0 %copy-start.2 = (f32[16,128]{1,0:T(8,128)S(1)}, f32[16,128]{1,0:T(8,128)}, u32[]{:S(2)}) copy-start(f32[16,128]{1,0:T(8,128)} %widths_ref.1) | copy-start | bytes 24580
  2.4 12.0 %copy-start.3 = (f32[16,128]{1,0:T(8,128)S(1)}, f32[16,128]{1,0:T(8,128)}, u32[]{:S(2)}) copy-start(f32[16,128]{1,0:T(8,128)} %density_ref.1) | copy-start | bytes 24580
  2.4 12.0 %copy-start.4 = (f32[16,128]{1,0:T(8,128)S(1)}, f32[16,128]{1,0:T(8,128)}, u32[]{:S(2)}) copy-start(f32[16,128]{1,0:T(8,128)} %prefactor_ref.1) | copy-start | bytes 24580
  2.4 12.0 %copy-start.5 = (s32[16]{0:T(128)S(1)}, s32[16]{0:T(128)}, u32[]{:S(2)}) copy-start(s32[16]{0:T(128)} %padding_ref.1) | copy-start | bytes 196

commit v7 on v3

--- a/solution.py
+++ b/solution.py
@@ -40,7 +40,8 @@
     mine = pl.multiple_of(p * owned, owned)
     out_ref[pl.ds(mine, owned), 0:3, :] = coords_ref[:, 0]
     out_ref[pl.ds(mine, owned), 3:4, :] = charges_ref[...]
-    peers = [lax.rem(p + k, n) for k in range(1, n)]
+    offsets = sorted(range(1, n), key=lambda k: -min(k, n - k))
+    peers = [lax.rem(p + k, n) for k in offsets]
     greet([{"pair": q} for q in peers] + [{"sub": 1 - s}])
 
     def part(q):
@@ -54,7 +55,7 @@
     across = []
     for k in range(n - 1):
         out[k].wait_recv()
-        q = lax.rem(p + n - 1 - k, n)
+        q = lax.rem(p + n - offsets[k], n)
         copy = remote(part(q), part(q), core_send.at[k], core_recv.at[k], sub=1 - s)
         copy.start()
         across.append(copy)
@@ -99,7 +100,8 @@
     last_recv,
 ):
     p, m, s = (lax.axis_index(a) for a in ("pair", "mm", "sub"))
-    peers = [lax.rem(p + k, n) for k in range(1, n)] + [p]
+    offsets = sorted(range(1, n), key=lambda k: -min(k, n - k))
+    peers = [lax.rem(p + k, n) for k in offsets] + [p]
     others = [lax.rem(m + k, groups) for k in range(1, groups)]
     greet([{"pair": q} for q in peers[:-1]] + [{"sub": 1 - s}] + [{"mm": g} for g in others])
     across = [

time: 41.8 us -> 41.9 us (level)
  no operation moved by 1% of the time
where the time goes in v7:
time: 41.9 us; the launch traced here: 41.4 us
  Pallas kernels  37.6 us (90%)
  local copies, waits for them, and re-layouts  3.07 us (7%)
  between operations  0.75 us (2%)
    pallas_call x1, Pallas kernels, interactions(): pl.pallas_call(pair_kernel, out_shape=(jax.ShapeDtypeStruct((atoms.shape[...  15.1 us
    pallas_call x1, Pallas kernels, gather(): pl.pallas_call(functools.partial(gather_kernel, n), out_shape=jax.ShapeDt...  12 us
    pallas_call x1, Pallas kernels, reduce(): pl.pallas_call(functools.partial(reduce_kernel, n, groups), out_shape=(ja...  10.5 us
    unnamed x16, local copies, waits for them, and re-layouts  3.06 us

profile of v7, /device:TPU:0, one launch (start us, length us, event | category | flops | bytes accessed | tf_op | source)
XLA Modules:
  0.0 41.4 jit_solution(10279142045135299455)
XLA Ops:
  0.6 0.8 %copy.13.centers_ref = f32[16,3,128]{2,1,0:T(4,128)S(1)} copy(f32[16,3,128]{2,0,1:T(8,128)} %param.8) | data formatting | bytes 49152 | tf_op args[0]
  1.4 0.0 copy-start
  1.4 0.9 %copy.12.coords_ref = f32[64,1,3,128]{3,2,1,0:T(4,128)S(1)} copy(f32[64,1,3,128]{3,1,2,0:T(1,128)} %param.14) | data formatting | bytes 196608 | tf_op args[6]
  2.3 0.0 copy-done
  2.3 0.0 copy-start.1
  2.3 0.0 copy-start.2
  2.4 0.0 copy-start.3
  2.4 0.0 copy-start.4
  2.4 0.0 copy-start.5
  2.4 12.0 %shard_map.95.atoms_ref = f32[256,4,128]{2,1,0:T(4,128)S(1)} custom-call(f32[64,1,3,128]{3,2,1,0:T(4,128)S(1)} %copy.12.coords_ref, f32[64,1,128]{2,1,0:T(1,128)S(1)} %copy-done), custom_call_target="tpu_custom_call" | custom-call | tf_op jit(solution)/shard_map/pallas_call | solution.py:70
  14.4 0.0 copy-done.1
  14.4 0.0 copy-done.2
  14.4 0.0 copy-done.3
  14.4 0.0 copy-done.4
  14.5 0.0 copy-done.5
  14.5 15.1 %shard_map.96 = (f32[24,32,128]{2,1,0:T(8,128)S(1)}, f32[3,16,128]{2,1,0:T(8,128)S(1)}) custom-call(s32[16,1,16]{2,1,0:T(1,128)S(1)} %copy-done.1, s32[16]{0:T(128)S(1)} %copy-done.5, f32[16,3,128]{2,1,0:T(4,128)S(1)} %copy.13.centers_ref, f32[16,128]{1,0:T(8,128)S(1)} %copy-done.2, f32[16,128]{1,0:T(8,128)S(1)} %copy-done.3, f32[16,128]{1,0:T(8,128)S(1)} %copy-done.4, ...), custom_call_target="tpu_custom_call" | custom-call | tf_op jit(solution)/shard_map/pallas_call | solution.py:292
  29.6 10.5 %shard_map.97 = (f32[2,3,32,128]{3,2,1,0:T(8,128)S(1)}, f32[3,16,128]{2,1,0:T(8,128)S(1)}) custom-call(f32[4,2,3,32,128]{4,3,2,1,0:T(8,128)S(1)} %bitcast.4, f32[3,16,128]{2,1,0:T(8,128)S(1)} %get-tuple-element.7.tile_ref), custom_call_target="tpu_custom_call" | custom-call | tf_op jit(solution)/shard_map/pallas_call | solution.py:148
  40.1 0.7 %copy.15 = f32[64,1,3,128]{3,1,2,0:T(1,128)} copy(f32[64,1,3,128]{3,0,2,1:T(8,128)S(1)} %bitcast.7) | data formatting | bytes 196608
  40.8 0.6 %copy.17 = f32[16,3,128]{2,0,1:T(8,128)} copy(f32[16,3,128]{2,0,1:T(8,128)S(1)} %bitcast.6) | data formatting | bytes 49152
  (1 shorter events, 0.0 us)
Async XLA Ops:
  1.4 0.9 %copy-start = (f32[64,1,128]{2,1,0:T(1,128)S(1)}, f32[64,1,128]{2,1,0:T(1,128)}, u32[]{:S(2)}) copy-start(f32[64,1,128]{2,1,0:T(1,128)} %charges_ref.1) | copy-start | bytes 98308
  2.3 12.1 %copy-start.1 = (s32[16,1,16]{2,1,0:T(1,128)S(1)}, s32[16,1,16]{2,1,0:T(1,128)}, u32[]{:S(2)}) copy-start(s32[16,1,16]{2,1,0:T(1,128)} %pattern_ref.1) | copy-start | bytes 3076
  2.3 12.1 %copy-start.2 = (f32[16,128]{1,0:T(8,128)S(1)}, f32[16,128]{1,0:T(8,128)}, u32[]{:S(2)}) copy-start(f32[16,128]{1,0:T(8,128)} %widths_ref.1) | copy-start | bytes 24580
  2.4 12.1 %copy-start.3 = (f32[16,128]{1,0:T(8,128)S(1)}, f32[16,128]{1,0:T(8,128)}, u32[]{:S(2)}) copy-start(f32[16,128]{1,0:T(8,128)} %density_ref.1) | copy-start | bytes 24580
  2.4 12.1 %copy-start.4 = (f32[16,128]{1,0:T(8,128)S(1)}, f32[16,128]{1,0:T(8,128)}, u32[]{:S(2)}) copy-start(f32[16,128]{1,0:T(8,128)} %prefactor_ref.1) | copy-start | bytes 24580
  2.4 12.1 %copy-start.5 = (s32[16]{0:T(128)S(1)}, s32[16]{0:T(128)}, u32[]{:S(2)}) copy-start(s32[16]{0:T(128)} %padding_ref.1) | copy-start | bytes 196
